TPU v7x, 32 devices: a whole 2x2x4 slice. The times are simulated.
32 devices in a mesh: seq: 16 (over z, y, x), opt: 2 (over core).
Axes of the slice: x: 2, y: 2, z: 4, core: 2. Of those that a mesh axis runs over, the one named last changes fastest.
Arguments:
- features: bfloat16 [2, 2048, 1536], P('opt', 'seq'), may hold values from -6 to 6
- tile_mask: int32 [2, 2048], P('opt', 'seq'), may hold values from 0 to 1, as said below
- lengths: int32 [2, 4], replicated, may hold values from 1 to 1024, 2048 in all within a row
- owners: int32 [768], replicated, may hold values from 0 to 767, each once
- layer_blocks: float32 [768, 96, 96], P(('seq', 'opt')), may hold values from -0.21875 to 0.21875
- stat_left: float32 [768, 96, 96], P(('seq', 'opt')), as said below
- stat_right: float32 [768, 96, 96], P(('seq', 'opt')), as said below
- io_weights: float32 [1536, 2, 768], P(('seq', 'opt')), may hold values from -0.21875 to 0.21875
- io_first: float32 [1536, 2, 768], P(('seq', 'opt')), may hold values from -0.00048828125 to 0.00048828125
- io_second: float32 [1536, 2, 768], P(('seq', 'opt')), may hold values from 5.5650915e-09 to 2.2218046e-08
- vectors: float32 [19, 768], replicated, may hold values from -3 to 3, as said below
- vec_first: float32 [19, 768], replicated, may hold values from -0.0017089844 to 0.0017089844
- vec_second: float32 [19, 768], replicated, may hold values from 5.2900113e-08 to 2.1160045e-07
Outputs:
- grad_norm: float32 [], replicated
- error_sum: float32 [], replicated
- masked_count: float32 [], replicated
- block_grads: float32 [768, 96, 96], P(('seq', 'opt'))
- left_new: float32 [768, 96, 96], P(('seq', 'opt'))
- right_new: float32 [768, 96, 96], P(('seq', 'opt'))
- blocks_new: float32 [768, 96, 96], P(('seq', 'opt'))
- io_first_new: float32 [1536, 2, 768], P(('seq', 'opt'))
- io_second_new: float32 [1536, 2, 768], P(('seq', 'opt'))
- io_new: float32 [1536, 2, 768], P(('seq', 'opt'))
- vec_first_new: float32 [19, 768], replicated
- vec_second_new: float32 [19, 768], replicated
- vec_new: float32 [19, 768], replicated
Inputs may be any that keep to these rules, and one draw needn't show every extreme that they name: `tile_mask`: 1 marks a masked tile. `lengths`: the 4 slides of a micro-batch in order fill all 2048 tiles; the longest has half of 2048 tiles. `owners`: each natural block in exactly one slot. `stat_left`: symmetric positive definite. `stat_right`: symmetric positive definite. `vectors`: gains positive.
All inputs are finite; a program needn't handle non-finite values.
Results may differ from a plain program's by a relative error of at most 0.0006.
The roundings to bfloat16 on the way count: a program that leaves them out, or rounds other values in their place, can miss the bound.
Values may be sent and summed in bfloat16 or wider, within the bound.
No kernel may reach another device: no remote copies, remote signals or barrier semaphores. Data moves between devices by JAX's collectives and lax.ppermute only.
A program may use at most 256 MiB of HBM per device.

v0:
```python
from functools import partial
import math

import jax
import jax.numpy as jnp
import numpy as np
from jax import lax
from jax.sharding import PartitionSpec as P

D = 768
HEADS = 16
HEAD_DIM = 48
FF = 3072
FEAT = 1536
LAYERS = 1
BRANCHES = 5
SEG0 = 1024
BLOCK = 96
SLIDES = 4
NEWTON = 6
STEP = 10


norm_eps = 1e-05
clip_limit = 1.0
beta_one = 0.9
beta_two = 0.95
adam_eps = 1e-08
rate_adam = 0.01
rate_vector = 0.2
weight_decay = 0.05
beta_stat = 0.95
rate_shampoo = 0.05
root_eps = 1e-12
masked_score = -1e30
highest = lax.Precision.HIGHEST


def from_partner(value, axis, stride):
    mask = 2**stride
    pairs = [(source, source ^ mask) for source in range(lax.axis_size(axis))]
    return lax.ppermute(value, axis, pairs)


def for_sending(shard):

    def short(part):
        return part.astype(jnp.bfloat16) if part.dtype == jnp.float32 else part

    return jax.tree.map(short, shard)


def layer_norm(values, gain, shift):
    centred = values - jnp.mean(values, axis=-1, keepdims=True)
    spread = jnp.mean(centred * centred, axis=-1, keepdims=True)
    return centred * lax.rsqrt(spread + norm_eps) * gain + shift


def sine_places(places):
    half_width = D // 2
    freq_rates = jnp.exp(
        jnp.arange(half_width, dtype=jnp.float32) * (-math.log(10000.0) / half_width)
    )
    angles = (places.astype(jnp.float32) / 64.0)[:, None] * freq_rates[None, :]
    return jnp.concatenate([jnp.sin(angles), jnp.cos(angles)], axis=1)


def slide_ids(lengths_row, places):
    slide_ends = jnp.cumsum(lengths_row)
    return jnp.sum((places[..., None] >= slide_ends[:-1]).astype(jnp.int32), axis=-1)


def slide_offsets(lengths_row, places):
    slide_ends = jnp.cumsum(lengths_row)
    slide_starts = slide_ends - lengths_row
    owner_ids = slide_ids(lengths_row, places)
    match_rows = owner_ids[:, None] == jnp.arange(SLIDES, dtype=jnp.int32)[None, :]
    picked = jnp.sum(jnp.where(match_rows, slide_starts[None, :], 0), axis=1)
    return places - picked


def head_offsets(dilation):
    return np.arange(HEADS) % dilation


def pick_rows(values, dilation):
    row_count = values.shape[0] // dilation
    shaped = values.reshape((row_count, dilation) + values.shape[1:])
    return shaped[:, head_offsets(dilation), np.arange(HEADS)]


def spread_rows(values, dilation, filler):
    row_count = values.shape[0]
    hit_mask = np.arange(dilation)[:, None] == head_offsets(dilation)[None, :]
    hit_mask = hit_mask.reshape((1, dilation, HEADS) + (1,) * (values.ndim - 2))
    spread_out = jnp.where(hit_mask, values[:, None], filler)
    return spread_out.reshape((row_count * dilation,) + values.shape[1:])


def branch_geom(branch, tok_dev, seq_len):
    dilation = 2**branch
    segment = min(SEG0 * dilation, seq_len)
    return (dilation, segment, max(1, segment // tok_dev))


def branch_docs(lengths_row, first_place, row_count, dilation):
    places = (
        first_place
        + jnp.asarray(head_offsets(dilation), jnp.int32)[None, :]
        + dilation * jnp.arange(row_count, dtype=jnp.int32)[:, None]
    )
    return slide_ids(lengths_row, places)


def contract_rows(left, right):
    return lax.dot_general(
        left, right, (((0,), (0,)), ((), ())), preferred_element_type=jnp.float32
    )


def contract_cols(left, right):
    return lax.dot_general(
        left, right, (((1,), (1,)), ((), ())), preferred_element_type=jnp.float32
    )


def assemble(natural):
    per_layer = natural.reshape(LAYERS, -1, BLOCK, BLOCK)
    col_count = (4 * D + FF) // BLOCK
    wide_count = D // BLOCK * col_count
    upper_mats = per_layer[:, :wide_count].reshape(LAYERS, D // BLOCK, col_count, BLOCK, BLOCK)
    upper_mats = upper_mats.transpose(0, 1, 3, 2, 4).reshape(LAYERS, D, 4 * D + FF)
    lower_mats = per_layer[:, wide_count:].reshape(LAYERS, FF // BLOCK, D // BLOCK, BLOCK, BLOCK)
    lower_mats = lower_mats.transpose(0, 1, 3, 2, 4).reshape(LAYERS, FF, D)
    return (upper_mats, lower_mats)


def disassemble(upper_mats, lower_mats):
    col_count = (4 * D + FF) // BLOCK
    top_part = upper_mats.reshape(LAYERS, D // BLOCK, BLOCK, col_count, BLOCK).transpose(
        0, 1, 3, 2, 4
    )
    top_part = top_part.reshape(LAYERS, -1, BLOCK, BLOCK)
    bottom_part = lower_mats.reshape(LAYERS, FF // BLOCK, BLOCK, D // BLOCK, BLOCK).transpose(
        0, 1, 3, 2, 4
    )
    bottom_part = bottom_part.reshape(LAYERS, -1, BLOCK, BLOCK)
    return jnp.concatenate([top_part, bottom_part], axis=1).reshape(-1, BLOCK, BLOCK)


def unpack(vector_set):
    per_layer = 8 + FF // D
    return (
        vector_set[: LAYERS * per_layer].reshape(LAYERS, per_layer, D),
        vector_set[LAYERS * per_layer :],
    )


def collect_pairs(pieces, bit_counts, seq_index):
    pieces = list(pieces)
    for bit_id in range(max(bit_counts + [0])):
        active_ids = [branch for branch in range(len(pieces)) if bit_counts[branch] > bit_id]
        outgoing = jnp.concatenate([pieces[branch] for branch in active_ids], axis=0)
        partner = from_partner(outgoing, "seq", bit_id)
        lower_side = seq_index // 2**bit_id % 2 == 0
        offset_at = 0
        for branch in active_ids:
            my_part = pieces[branch]
            part_size = my_part.shape[0]
            their_part = partner[offset_at : offset_at + part_size]
            offset_at = offset_at + part_size
            pieces[branch] = jnp.where(
                lower_side,
                jnp.concatenate([my_part, their_part], 0),
                jnp.concatenate([their_part, my_part], 0),
            )
    return pieces


def return_pairs(pieces, bit_counts, seq_index):
    pieces = list(pieces)
    for bit_id in reversed(range(max(bit_counts + [0]))):
        active_ids = [branch for branch in range(len(pieces)) if bit_counts[branch] > bit_id]
        lower_side = seq_index // 2**bit_id % 2 == 0
        kept_parts, sent_parts = ([], [])
        for branch in active_ids:
            half_size = pieces[branch].shape[0] // 2
            first_part = pieces[branch][:half_size]
            second_part = pieces[branch][half_size:]
            kept_parts.append(jnp.where(lower_side, first_part, second_part))
            sent_parts.append(jnp.where(lower_side, second_part, first_part))
        partner = from_partner(for_sending(jnp.concatenate(sent_parts, axis=0)), "seq", bit_id)
        offset_at = 0
        for branch, kept_part in zip(active_ids, kept_parts):
            part_size = kept_part.shape[0]
            pieces[branch] = kept_part + partner[offset_at : offset_at + part_size]
            offset_at = offset_at + part_size
    return pieces


def score_block(query_rows, key_rows, query_docs, key_docs):
    raw_scores = jnp.einsum(
        "sqhd,skhd->shqk", query_rows, key_rows, preferred_element_type=jnp.float32
    ) * HEAD_DIM ** (-0.5)
    same_slide = (
        jnp.transpose(query_docs, (0, 2, 1))[..., None]
        == jnp.transpose(key_docs, (0, 2, 1))[:, :, None, :]
    )
    return jnp.where(same_slide, raw_scores, masked_score)


def attend_forward(packed, lengths_row, seq_len, seq_index):
    tok_dev = packed.shape[0]
    triple = packed.reshape(tok_dev, 3, HEADS, HEAD_DIM)
    queries, key_all, value_all = (triple[:, 0], triple[:, 1], triple[:, 2])
    geoms = [branch_geom(branch, tok_dev, seq_len) for branch in range(BRANCHES)]
    local_pairs = [
        jnp.stack([pick_rows(key_all, geom[0]), pick_rows(value_all, geom[0])], axis=1).reshape(
            -1, 2 * D
        )
        for geom in geoms
    ]
    bit_counts = [geom[2].bit_length() - 1 for geom in geoms]
    joined = collect_pairs(local_pairs, bit_counts, seq_index)
    kept_state, outputs, totals_all = ([], [], [])
    for branch in range(BRANCHES):
        dilation, segment, group_size = geoms[branch]
        sections = max(1, tok_dev // segment)
        query_rows = pick_rows(queries, dilation).reshape(sections, -1, HEADS, HEAD_DIM)
        pair_rows = joined[branch].reshape(sections, -1, 2, HEADS, HEAD_DIM)
        key_rows = pair_rows[:, :, 0]
        value_rows = pair_rows[:, :, 1]
        query_docs = branch_docs(
            lengths_row, seq_index * tok_dev, tok_dev // dilation, dilation
        ).reshape(sections, -1, HEADS)
        group_first = seq_index // group_size * group_size * tok_dev
        key_docs = branch_docs(lengths_row, group_first, joined[branch].shape[0], dilation).reshape(
            sections, -1, HEADS
        )
        scores = score_block(query_rows, key_rows, query_docs, key_docs)
        totals = jax.nn.logsumexp(scores, axis=-1)
        softmax_rows = jnp.exp(scores - totals[..., None]).astype(jnp.bfloat16)
        output = jnp.einsum(
            "shqk,skhd->sqhd", softmax_rows, value_rows, preferred_element_type=jnp.float32
        ).reshape(-1, HEADS, HEAD_DIM)
        totals_rows = jnp.transpose(totals, (0, 2, 1)).reshape(-1, HEADS)
        kept_state.append(
            (query_rows, key_rows, value_rows, query_docs, key_docs, output, totals_rows)
        )
        outputs.append(spread_rows(output, dilation, 0.0))
        totals_all.append(spread_rows(totals_rows, dilation, masked_score))
    stacked = jnp.stack(totals_all)
    grand_total = jax.nn.logsumexp(stacked, axis=0)
    mixed_out = jnp.zeros_like(outputs[0])
    for branch in range(BRANCHES):
        mixed_out = mixed_out + jnp.exp(stacked[branch] - grand_total)[..., None] * outputs[branch]
    return (mixed_out, (mixed_out, grand_total, kept_state))


def attend_backward(grad_mixed, attention_state, seq_len, seq_index):
    mixed_out, grand_total, kept_state = attention_state
    tok_dev = grad_mixed.shape[0]
    score_scale = HEAD_DIM ** (-0.5)
    grad_query = jnp.zeros(grad_mixed.shape, jnp.float32)
    key_terms, bit_counts, dilations = ([], [], [])
    for branch in range(BRANCHES):
        dilation, segment, group_size = branch_geom(branch, tok_dev, seq_len)
        query_rows, key_rows, value_rows, query_docs, key_docs, output, totals_rows = kept_state[
            branch
        ]
        sections = query_rows.shape[0]
        weight = jnp.exp(totals_rows - pick_rows(grand_total, dilation))
        grad_picked = pick_rows(grad_mixed, dilation)
        grad_output = (
            (weight[..., None] * grad_picked)
            .astype(jnp.bfloat16)
            .reshape(sections, -1, HEADS, HEAD_DIM)
        )
        grad_totals = weight * jnp.sum(
            grad_picked * (output - pick_rows(mixed_out, dilation)), axis=-1
        )
        grad_totals = jnp.transpose(grad_totals.reshape(sections, -1, HEADS), (0, 2, 1))
        totals = jnp.transpose(totals_rows.reshape(sections, -1, HEADS), (0, 2, 1))
        softmax_rows = jnp.exp(
            score_block(query_rows, key_rows, query_docs, key_docs) - totals[..., None]
        )
        grad_value = jnp.einsum(
            "shqk,sqhd->skhd",
            softmax_rows.astype(jnp.bfloat16),
            grad_output,
            preferred_element_type=jnp.float32,
        )
        grad_probs = jnp.einsum(
            "sqhd,skhd->shqk", grad_output, value_rows, preferred_element_type=jnp.float32
        )
        inner_sum = jnp.sum(softmax_rows * grad_probs, axis=-1, keepdims=True)
        grad_scores = (softmax_rows * (grad_probs - inner_sum + grad_totals[..., None])).astype(
            jnp.bfloat16
        )
        grad_q = (
            jnp.einsum("shqk,skhd->sqhd", grad_scores, key_rows, preferred_element_type=jnp.float32)
            * score_scale
        )
        grad_k = (
            jnp.einsum(
                "shqk,sqhd->skhd", grad_scores, query_rows, preferred_element_type=jnp.float32
            )
            * score_scale
        )
        grad_query = grad_query + spread_rows(grad_q.reshape(-1, HEADS, HEAD_DIM), dilation, 0.0)
        key_terms.append(
            jnp.stack(
                [grad_k.reshape(-1, HEADS, HEAD_DIM), grad_value.reshape(-1, HEADS, HEAD_DIM)],
                axis=1,
            ).reshape(-1, 2 * D)
        )
        bit_counts.append(group_size.bit_length() - 1)
        dilations.append(dilation)
    own_terms = return_pairs(key_terms, bit_counts, seq_index)
    grad_key = jnp.zeros(grad_mixed.shape, jnp.float32)
    grad_val = jnp.zeros(grad_mixed.shape, jnp.float32)
    for branch in range(BRANCHES):
        pair_rows = own_terms[branch].reshape(-1, 2, HEADS, HEAD_DIM)
        grad_key = grad_key + spread_rows(pair_rows[:, 0], dilations[branch], 0.0)
        grad_val = grad_val + spread_rows(pair_rows[:, 1], dilations[branch], 0.0)
    return jnp.stack([grad_query, grad_key, grad_val], axis=1).reshape(tok_dev, 3 * D)


def layer_forward(hidden, upper_mat, lower_mat, row_set, lengths_row, seq_len, seq_index):
    normed = layer_norm(hidden, row_set[0], row_set[1]).astype(jnp.bfloat16)
    biases = jnp.concatenate([row_set[2], jnp.zeros_like(row_set[2]), row_set[3]])
    packed = (
        jnp.dot(normed, upper_mat[:, : 3 * D], preferred_element_type=jnp.float32) + biases[None, :]
    ).astype(jnp.bfloat16)
    mixed_out, attention_state = attend_forward(packed, lengths_row, seq_len, seq_index)
    mixed_low = mixed_out.reshape(-1, D).astype(jnp.bfloat16)
    middle = (
        hidden
        + jnp.dot(mixed_low, upper_mat[:, 3 * D : 4 * D], preferred_element_type=jnp.float32)
        + row_set[4][None, :]
    )
    second = layer_norm(middle, row_set[5], row_set[6]).astype(jnp.bfloat16)
    before = (
        jnp.dot(second, upper_mat[:, 4 * D :], preferred_element_type=jnp.float32)
        + row_set[8:].reshape(-1)[None, :]
    )
    active = jax.nn.gelu(before, approximate=True).astype(jnp.bfloat16)
    result = (
        middle
        + jnp.dot(active, lower_mat, preferred_element_type=jnp.float32)
        + row_set[7][None, :]
    )
    return (result, (hidden, normed, mixed_low, middle, second, before, active, attention_state))


def layer_backward(grad_result, upper_mat, lower_mat, row_set, layer_state, seq_len, seq_index):
    hidden, normed, mixed_low, middle, second, before, active, attention_state = layer_state
    grad_out = grad_result.astype(jnp.bfloat16)
    grad_lower = contract_rows(active, grad_out)
    grad_fc2_bias = jnp.sum(grad_out, axis=0, dtype=jnp.float32)
    grad_active = contract_cols(grad_out, lower_mat)
    gelu_value, gelu_back = jax.vjp(partial(jax.nn.gelu, approximate=True), before)
    grad_before = gelu_back(grad_active)[0].astype(jnp.bfloat16)
    grad_fc1 = contract_rows(second, grad_before)
    grad_fc1_bias = jnp.sum(grad_before, axis=0, dtype=jnp.float32)
    grad_second = contract_cols(grad_before, upper_mat[:, 4 * D :])
    norm_value, norm_back = jax.vjp(layer_norm, middle, row_set[5], row_set[6])
    grad_middle, grad_gain_two, grad_shift_two = norm_back(grad_second)
    grad_middle = grad_middle + grad_result
    grad_branch = grad_middle.astype(jnp.bfloat16)
    grad_proj = contract_rows(mixed_low, grad_branch)
    grad_proj_bias = jnp.sum(grad_branch, axis=0, dtype=jnp.float32)
    grad_mixed = contract_cols(grad_branch, upper_mat[:, 3 * D : 4 * D]).reshape(
        -1, HEADS, HEAD_DIM
    )
    grad_packed = attend_backward(grad_mixed, attention_state, seq_len, seq_index).astype(
        jnp.bfloat16
    )
    grad_qkv = contract_rows(normed, grad_packed)
    packed_sums = jnp.sum(grad_packed, axis=0, dtype=jnp.float32)
    grad_normed = contract_cols(grad_packed, upper_mat[:, : 3 * D])
    first_value, first_back = jax.vjp(layer_norm, hidden, row_set[0], row_set[1])
    grad_hidden, grad_gain_one, grad_shift_one = first_back(grad_normed)
    grad_hidden = grad_hidden + grad_middle
    grad_upper = jnp.concatenate([grad_qkv, grad_proj, grad_fc1], axis=1)
    small_rows = jnp.stack(
        [
            grad_gain_one,
            grad_shift_one,
            packed_sums[:D],
            packed_sums[2 * D :],
            grad_proj_bias,
            grad_gain_two,
            grad_shift_two,
            grad_fc2_bias,
        ]
    )
    grad_rows = jnp.concatenate([small_rows, grad_fc1_bias.reshape(-1, D)], axis=0)
    return (grad_hidden, (grad_upper, grad_lower, grad_rows))


def inverse_root(matrix):
    identity = jnp.eye(matrix.shape[-1], dtype=jnp.float32)
    regular = matrix + root_eps * identity
    frob_norm = jnp.sqrt(jnp.sum(regular * regular, axis=(1, 2), keepdims=True))
    scaled = 2.5 / frob_norm
    root_mat = identity * jnp.sqrt(jnp.sqrt(scaled))
    moving = regular * scaled
    for sweep_id in range(NEWTON):
        factor = (5.0 * identity - moving) * 0.25
        root_mat = jnp.einsum("kij,kjl->kil", root_mat, factor, precision=highest)
        square = jnp.einsum("kij,kjl->kil", factor, factor, precision=highest)
        fourth = jnp.einsum("kij,kjl->kil", square, square, precision=highest)
        moving = jnp.einsum("kij,kjl->kil", fourth, moving, precision=highest)
    return root_mat


def adam_update(weight, first_mom, second_mom, grad, rate, decay):
    first_new = beta_one * first_mom + (1.0 - beta_one) * grad
    second_new = beta_two * second_mom + (1.0 - beta_two) * grad * grad
    first_hat = first_new / (1.0 - beta_one**STEP)
    second_hat = second_new / (1.0 - beta_two**STEP)
    return (
        first_new,
        second_new,
        weight - rate * (first_hat / (jnp.sqrt(second_hat) + adam_eps) + decay * weight),
    )


def per_device(
    features,
    tile_mask,
    lengths,
    owners,
    layer_blocks,
    stat_left,
    stat_right,
    io_weights,
    io_first,
    io_second,
    vectors,
    vec_first,
    vec_second,
):
    tok_dev = features.shape[1]
    seq_size = lax.axis_size("seq")
    seq_len = tok_dev * seq_size
    seq_index = lax.axis_index("seq")
    core_index = lax.axis_index("opt")
    targets = features[0].astype(jnp.float32)
    chosen = tile_mask[0][:, None] > 0
    lengths_row = lax.dynamic_index_in_dim(lengths, core_index, 0, keepdims=False)
    places = seq_index * tok_dev + jnp.arange(tok_dev, dtype=jnp.int32)
    all_blocks, all_io = (
        lax.all_gather(layer_blocks.astype(jnp.bfloat16), ("seq", "opt"), axis=0, tiled=True),
        lax.all_gather(io_weights.astype(jnp.bfloat16), ("seq", "opt"), axis=0, tiled=True),
    )
    natural = jnp.zeros_like(all_blocks).at[owners].set(all_blocks)
    upper_mats, lower_mats = assemble(natural)
    tile_count = lax.psum(jnp.sum(tile_mask.astype(jnp.float32)), ("seq", "opt"))
    layer_rows, tail_rows = unpack(vectors)
    token_vec = tail_rows[3 + FEAT // D :].reshape(FEAT)
    head_bias = tail_rows[3 : 3 + FEAT // D].reshape(FEAT)
    inputs = jnp.where(chosen, token_vec[None, :], targets).astype(jnp.bfloat16)
    in_weight = all_io[:, 0]
    head_weight = all_io[:, 1]
    hidden = jnp.dot(inputs, in_weight, preferred_element_type=jnp.float32) + tail_rows[2][None, :]
    hidden = hidden + sine_places(slide_offsets(lengths_row, places))
    layer_id = 0
    hidden, layer_state = layer_forward(
        hidden,
        upper_mats[layer_id],
        lower_mats[layer_id],
        layer_rows[layer_id],
        lengths_row,
        seq_len,
        seq_index,
    )
    layer_states = [layer_state]
    final, final_back = jax.vjp(layer_norm, hidden, tail_rows[0], tail_rows[1])
    final_low = final.astype(jnp.bfloat16)
    predict = contract_cols(final_low, head_weight) + head_bias[None, :]
    difference = predict - targets
    error_local = jnp.sum(jnp.where(chosen, difference * difference, 0.0))
    grad_pred = jnp.where(chosen, 2.0 * difference / tile_count, 0.0).astype(jnp.bfloat16)
    grad_head = contract_rows(grad_pred, final_low)
    grad_head_bias = jnp.sum(grad_pred, axis=0, dtype=jnp.float32)
    grad_final = jnp.dot(grad_pred, head_weight, preferred_element_type=jnp.float32)
    grad_hidden, grad_gain_last, grad_shift_last = final_back(grad_final)
    layer_grads = [None] * LAYERS
    for layer_id in reversed(range(LAYERS)):
        grad_hidden, layer_grads[layer_id] = layer_backward(
            grad_hidden,
            upper_mats[layer_id],
            lower_mats[layer_id],
            layer_rows[layer_id],
            layer_states[layer_id],
            seq_len,
            seq_index,
        )
    grad_in_low = grad_hidden.astype(jnp.bfloat16)
    grad_in = contract_rows(inputs, grad_in_low)
    grad_in_bias = jnp.sum(grad_in_low, axis=0, dtype=jnp.float32)
    grad_inputs = contract_cols(grad_in_low, in_weight)
    grad_token = jnp.sum(jnp.where(chosen, grad_inputs, 0.0), axis=0)
    grad_upper = jnp.stack([item[0] for item in layer_grads])
    grad_lower = jnp.stack([item[1] for item in layer_grads])
    slot_grads = disassemble(grad_upper, grad_lower)[owners]
    io_grads = jnp.stack([grad_in, grad_head], axis=1)
    vec_grads = jnp.concatenate(
        [
            jnp.stack([item[2] for item in layer_grads]).reshape(-1, D),
            jnp.stack([grad_gain_last, grad_shift_last, grad_in_bias]),
            grad_head_bias.reshape(-1, D),
            grad_token.reshape(-1, D),
        ],
        axis=0,
    )
    slot_sum, io_sum = (
        lax.psum_scatter(slot_grads, ("seq", "opt"), scatter_dimension=0, tiled=True),
        lax.psum_scatter(io_grads, ("seq", "opt"), scatter_dimension=0, tiled=True),
    )
    vec_sum, error_sum = lax.psum((vec_grads, error_local), ("seq", "opt"))
    local_sq = jnp.sum(slot_sum * slot_sum) + jnp.sum(io_sum * io_sum)
    grad_norm = jnp.sqrt(lax.psum(local_sq, ("seq", "opt")) + jnp.sum(vec_sum * vec_sum))
    factor = jnp.minimum(1.0, clip_limit / grad_norm)
    block_grads = slot_sum * factor
    left_new = beta_stat * stat_left + (1.0 - beta_stat) * jnp.einsum(
        "kij,klj->kil", block_grads, block_grads, precision=highest
    )
    right_new = beta_stat * stat_right + (1.0 - beta_stat) * jnp.einsum(
        "kji,kjl->kil", block_grads, block_grads, precision=highest
    )
    direction = jnp.einsum("kij,kjl->kil", inverse_root(left_new), block_grads, precision=highest)
    direction = jnp.einsum("kij,kjl->kil", direction, inverse_root(right_new), precision=highest)
    blocks_new = layer_blocks - rate_shampoo * direction
    io_first_new, io_second_new, io_new = adam_update(
        io_weights, io_first, io_second, io_sum * factor, rate_adam, weight_decay
    )
    vec_first_new, vec_second_new, vec_new = adam_update(
        vectors, vec_first, vec_second, vec_sum * factor, rate_vector, 0.0
    )
    return (
        grad_norm,
        error_sum,
        tile_count,
        block_grads,
        left_new,
        right_new,
        blocks_new,
        io_first_new,
        io_second_new,
        io_new,
        vec_first_new,
        vec_second_new,
        vec_new,
    )


def solution(mesh):
    return jax.shard_map(
        per_device,
        mesh=mesh,
        in_specs=(
            P("opt", "seq", None),
            P("opt", "seq"),
            P(),
            P(),
            P(("seq", "opt"), None, None),
            P(("seq", "opt"), None, None),
            P(("seq", "opt"), None, None),
            P(("seq", "opt"), None, None),
            P(("seq", "opt"), None, None),
            P(("seq", "opt"), None, None),
            P(),
            P(),
            P(),
        ),
        out_specs=(
            P(),
            P(),
            P(),
            P(("seq", "opt"), None, None),
            P(("seq", "opt"), None, None),
            P(("seq", "opt"), None, None),
            P(("seq", "opt"), None, None),
            P(("seq", "opt"), None, None),
            P(("seq", "opt"), None, None),
            P(("seq", "opt"), None, None),
            P(),
            P(),
            P(),
        ),
        check_vma=False,
    )
```

profile of v0, /device:TPU:0, one launch (start us, length us, event | category | flops | bytes accessed | tf_op | source)
XLA Modules:
  0.0 2021.5 jit_solution(10988416786393315818)
XLA Ops:
  13.8 64.1 %all-gather.3.cloned.1.call-done = bf16[1536,2,768]{2,0,1:T(8,128)(2,1)} async-done(((bf16[48,2,768]{2,0,1:T(8,128)(2,1)}), bf16[1536,2,768]{2,0,1:T(8,128)(2,1)}) %all-gather.3.cloned.1.call-update) | async-done | bytes 4718608 | tf_op jit(solution)/shard_map/all_gather | solution.py:456
  80.5 124.4 %all-gather.5.cloned.1.call-done = bf16[768,96,96]{2,1,0:T(8,128)(2,1)} async-done(((bf16[24,96,96]{2,1,0:T(8,128)(2,1)}), bf16[768,96,96]{2,1,0:T(8,128)(2,1)}) %all-gather.5.cloned.1.call-update) | async-done | bytes 14155792 | tf_op jit(solution)/shard_map/all_gather | solution.py:455
  205.0 6.8 broadcast_in_dim.1191
  211.7 104.2 %scatter_fusion = bf16[768,96,96]{2,1,0:T(8,128)(2,1)} fusion(bf16[768,96,96]{2,1,0:T(8,128)(2,1)} %broadcast_in_dim.1191, s32[768]{0:T(1024)S(1)} %compare_select_fusion, bf16[768,96,96]{2,1,0:T(8,128)(2,1)} %all-gather.5.cloned.1.call-done), kind=kCustom, calls=%fused_computation.31 | custom fusion | bytes 42470400 | tf_op jit(solution)/shard_map/scatter | solution.py:458
  315.9 6.9 slice.599
  322.8 15.7 copy.1927
  338.5 23.0 %squeeze_reshape.8 = bf16[768,6144]{1,0:T(8,128)(2,1)} reshape(bf16[1,8,96,64,96]{4,3,2,1,0:T(8,128)(2,1)} %bitcast.962) | data formatting | bytes 18874368 | tf_op jit(solution)/shard_map/squeeze;reshape | solution.py:472
  361.6 2.7 fusion.17
  382.3 15.5 collective-permute-done
  400.7 32.8 %collective-permute-done.1 = bf16[496,1536]{1,0:T(8,128)(2,1)S(1)} collective-permute-done((bf16[496,1536]{1,0:T(8,128)(2,1)S(1)}, bf16[496,1536]{1,0:T(8,128)(2,1)S(1)}, u32[]{:S(2)}, u32[]{:S(2)}) %collective-permute-start.1) | collective-permute-done | bytes 1523744 | tf_op jit(solution)/shard_map/ppermute | solution.py:42
  440.0 85.9 %psum.28 = f32[]{:T(128)} all-reduce(f32[]{:T(128)} %convert_reduce_fusion.17), channel_id=1, replica_groups=mesh['seq'=16,'opt'=2] {'seq','opt'}, use_global_device_ids=true, to_apply=%region_32.33 | all-reduce | flops 1 | bytes 8 | tf_op jit(solution)/shard_map/psum | solution.py:460
  545.9 6.5 slice.635
  566.3 8.4 copy.1928
  574.7 11.0 squeeze_reshape.9
  638.5 2.9 exponential_reduce_fusion
  642.5 100.9 %collective-permute-done.3 = bf16[960,1536]{1,0:T(8,128)(2,1)} collective-permute-done((bf16[960,1536]{1,0:T(8,128)(2,1)}, bf16[960,1536]{1,0:T(8,128)(2,1)}, u32[]{:S(2)}, u32[]{:S(2)}) %collective-permute-start.3) | collective-permute-done | bytes 2949152 | tf_op jit(solution)/shard_map/ppermute | solution.py:42
  761.0 4.1 maximum_select_fusion.1
  825.1 3.8 fusion.85
  853.5 7.5 fusion.277
  863.8 3.2 fusion.14
  867.1 4.2 fusion.478
  871.7 4.9 convert_reduce_fusion.2
  897.7 2.8 copy.1786
  905.8 2.7 copy.1706
  910.3 4.4 fusion.76
  949.8 2.9 multiply_add_fusion
  959.2 4.4 fusion.153
  969.7 6.2 fusion.146
  990.5 7.1 fusion.138
  1002.5 12.7 multiply_bitcast_fusion
  1015.2 3.6 select_convert_fusion
  1018.8 3.0 copy.1811
  1021.8 5.8 multiply_bitcast_fusion.2
  1027.6 2.9 select_convert_fusion.4
  1032.8 3.4 fusion.83
  1047.0 3.2 pad_maximum_fusion.5
  1064.2 3.3 broadcast_select_fusion.2
  1067.5 3.0 copy.1816
  1070.5 4.4 broadcast_select_fusion
  1074.9 3.7 copy.1815
  1080.4 5.3 fusion.75
  1085.7 20.0 multiply_bitcast_fusion.1
  1105.7 5.8 fusion.51
  1116.8 62.3 %collective-permute-done.4 = bf16[960,1536]{1,0:T(8,128)(2,1)} collective-permute-done((bf16[960,1536]{1,0:T(8,128)(2,1)}, bf16[960,1536]{1,0:T(8,128)(2,1)}, u32[]{:S(2)}, u32[]{:S(2)}) %collective-permute-start.4) | collective-permute-done | bytes 2949152 | tf_op jit(solution)/shard_map/ppermute | solution.py:42
  1192.2 3.6 copy.1820
  1195.8 62.2 %collective-permute-done.5 = bf16[992,1536]{1,0:T(8,128)(2,1)} collective-permute-done((bf16[992,1536]{1,0:T(8,128)(2,1)}, bf16[992,1536]{1,0:T(8,128)(2,1)}, u32[]{:S(2)}, u32[]{:S(2)}) %collective-permute-start.5) | collective-permute-done | bytes 3047456 | tf_op jit(solution)/shard_map/ppermute | solution.py:42
  1258.0 2.8 convert_add_fusion
  1272.3 5.1 fusion.123
  1277.5 11.3 fusion.100
  1288.8 16.5 collective-permute-done.6
  1333.5 4.2 convolution_bitcast_fusion
  1337.7 26.8 %fusion.112 = bf16[128,1,16,48]{0,3,2,1:T(8,128)(2,1)} fusion(f32[16,128,1024]{2,1,0:T(8,128)} %fusion.75, f32[16,128]{1,0:T(8,128)} %fusion.390, bf16[1,1024,2,16,48]{1,4,3,2,0:T(8,128)(2,1)} %copy-done.28, f32[128,1,16,48]{0,3,2,1:T(8,128)} %copy.1810, f32[128,1,16,48]{0,3,2,1:T(8,128)S(1)} %copy-done.167, f32[128,1,16,48]{0,3,2,1:T(8,128)S(1)} %copy-done.166, ...), kind=kOutput, calls=%fused_computation.187 | convolution fusion | flops 229575680 | bytes 37076992 | tf_op jit(solution)/shard_map/shqk,skhd->sqhd/dot_general | solution.py:301
  1386.2 3.5 multiply_reduce_fusion.9
  1391.7 4.2 pad_maximum_fusion.1
  1397.3 5.2 fusion.456
  1402.5 14.2 reshape_stack.7
  1416.7 12.2 copy.1832
  1433.0 6.8 pad_maximum_fusion
  1439.9 23.8 %reshape_stack.6 = f32[1,8,96,64,96]{4,3,2,1,0:T(8,128)} reshape(f32[768,6144]{1,0:T(8,128)} %pad_maximum_fusion) | data formatting | bytes 37748736 | tf_op jit(solution)/shard_map/reshape;stack | solution.py:140
  1463.6 25.2 %copy.1831 = f32[1,8,96,64,96]{4,2,3,1,0:T(8,128)} copy(f32[1,8,96,64,96]{4,3,2,1,0:T(8,128)} %reshape_stack.6) | data formatting | bytes 37748736 | tf_op jit(solution)/shard_map/reshape;stack | solution.py:140
  1488.8 27.7 %maximum_bitcast_fusion = f32[768,96,96]{2,1,0:T(8,128)} fusion(f32[1,256,96,96]{3,2,1,0:T(8,128)} %bitcast.960, f32[1,512,96,96]{3,2,1,0:T(8,128)} %bitcast.959), kind=kLoop, calls=%fused_computation.37 | loop fusion | flops 7077888 | bytes 56623104 | tf_op jit(solution)/shard_map/reshape | solution.py:148
  1516.5 29.5 %gather_fusion.30 = f32[768,96,96]{2,1,0:T(8,128)} fusion(f32[768,96,96]{2,1,0:T(8,128)} %maximum_bitcast_fusion, s32[1024]{0:T(1024)S(1)} %pad_clamp_fusion), kind=kCustom, calls=%fused_computation.30 | custom fusion | bytes 56626176 | tf_op jit(solution)/shard_map/gather | solution.py:508
  1551.6 343.0 %reduce-scatter.3.cloned.1.call-done = f32[24,96,96]{2,1,0:T(8,128)} async-done(((f32[768,96,96]{2,1,0:T(8,128)}), f32[24,96,96]{2,1,0:T(8,128)}) %reduce-scatter.3.cloned.1.call-update) | async-done | bytes 884752 | tf_op jit(solution)/shard_map/reduce_scatter | solution.py:520
  1898.1 40.7 %all-reduce = (f32[]{:T(128)}, f32[19,768]{1,0:T(8,128)S(1)}, f32[]{:T(128)}) all-reduce(f32[]{:T(128)S(6)} %add.1325, f32[19,768]{1,0:T(8,128)S(1)} %concatenate.661, f32[]{:T(128)} %get-tuple-element.191), channel_id=1, replica_groups=mesh['seq'=16,'opt'=2] {'seq','opt'}, use_global_device_ids=true, to_apply=%region_53.54 | all-reduce | flops 14594 | bytes 116752 | tf_op jit(solution)/shard_map/psum | solution.py:525
  (1299 shorter events, 517.7 us)
Async XLA Ops:
  7.2 70.8 %all-gather.3.cloned.1.call-start = ((), (), s32[]{:S(2)}) async-start(), calls=%async_computation.2 | async-start | bytes 4866048 | tf_op jit(solution)/shard_map/all_gather | solution.py:456
  8.9 69.1 %copy-start.161 = (bf16[1,128,1536]{2,1,0:T(8,128)(2,1)S(1)}, bf16[1,128,1536]{2,1,0:T(8,128)(2,1)}, u32[]{:S(2)}) copy-start(bf16[1,128,1536]{2,1,0:T(8,128)(2,1)} %param.168) | copy-start | bytes 1179652
  8.9 196.0 %all-gather.5.cloned.1.call-start = ((), (), s32[]{:S(2)}) async-start(), calls=%async_computation.3 | async-start | bytes 19464192 | tf_op jit(solution)/shard_map/all_gather | solution.py:455
  11.2 1538.7 %reduce-scatter.5.cloned.1.call-start = ((), (), s32[]{:S(2)}) async-start(), calls=%async_computation.5 | async-start | bytes 9732096 | tf_op jit(solution)/shard_map/reduce_scatter | solution.py:521
  11.5 68.7 %copy-start.287 = (bf16[1536]{0:T(1024)(128)(2,1)}, bf16[1536]{0:T(1024)(128)(2,1)S(1)}, u32[]{:S(2)}) copy-start(bf16[1536]{0:T(1024)(128)(2,1)S(1)} %broadcast_in_dim.1184) | copy-start | bytes 9220
  11.6 548.9 %copy-start.45 = (s32[16]{0:T(128)}, s32[16]{0:T(128)S(1)}, u32[]{:S(2)}) copy-start(s32[16]{0:T(128)S(1)} %or_bitcast_fusion) | copy-start | bytes 196
  12.8 348.7 %copy-start.198 = (f32[768]{0:T(1024)}, f32[768]{0:T(1024)S(1)}, u32[]{:S(2)}) copy-start(f32[768]{0:T(1024)S(1)} %get-tuple-element.122) | copy-start | bytes 9220
  12.8 348.7 %copy-start.232 = (f32[768]{0:T(1024)}, f32[768]{0:T(1024)S(1)}, u32[]{:S(2)}) copy-start(f32[768]{0:T(1024)S(1)} %get-tuple-element.121) | copy-start | bytes 9220
  12.8 387.7 %copy-start.268 = (s32[3]{0:T(128)}, s32[3]{0:T(128)S(1)}, u32[]{:S(2)}) copy-start(s32[3]{0:T(128)S(1)} %slice_bitcast_fusion.68) | copy-start | bytes 40
  13.0 67.2 %copy-start.324 = (pred[128]{0:T(512)(128)(4,1)}, pred[128]{0:T(512)(128)(4,1)S(1)}, u32[]{:S(2)}) copy-start(pred[128]{0:T(512)(128)(4,1)S(1)} %compare_bitcast_fusion) | copy-start | bytes 388
  13.1 198.7 %copy-start.252 = (s32[768]{0:T(1024)}, s32[768]{0:T(1024)S(1)}, u32[]{:S(2)}) copy-start(s32[768]{0:T(1024)S(1)} %compare_select_fusion) | copy-start | bytes 9220
  80.3 781.4 %copy-start.22 = (f32[128,768]{1,0:T(8,128)}, f32[128,768]{1,0:T(8,128)S(1)}, u32[]{:S(2)}) copy-start(f32[128,768]{1,0:T(8,128)S(1)} %get-tuple-element.242) | copy-start | bytes 1179652
  80.3 281.3 %copy-start.299 = (f32[128]{0:T(128)}, f32[128]{0:T(128)S(1)}, u32[]{:S(2)}) copy-start(f32[128]{0:T(128)S(1)} %broadcast_multiply_fusion.3) | copy-start | bytes 1540
  80.5 131.3 %copy-start.327 = (f32[128]{0:T(128)}, f32[128]{0:T(128)S(1)}, u32[]{:S(2)}) copy-start(f32[128]{0:T(128)S(1)} %multiply_reduce_fusion.15) | copy-start | bytes 1540
  80.5 281.0 %copy-start.311 = (f32[128]{0:T(128)}, f32[128]{0:T(128)S(1)}, u32[]{:S(2)}) copy-start(f32[128]{0:T(128)S(1)} %fusion.426) | copy-start | bytes 1540
  378.6 19.2 collective-permute-start
  398.1 35.5 %copy-start.92 = (bf16[64,1536]{1,0:T(8,128)(2,1)}, bf16[64,1536]{1,0:T(8,128)(2,1)S(1)}, u32[]{:S(2)}) copy-start(bf16[64,1536]{1,0:T(8,128)(2,1)S(1)} %slice.604) | copy-start | bytes 589828
  398.2 35.4 %copy-start.141 = (bf16[32,1536]{1,0:T(8,128)(2,1)}, bf16[32,1536]{1,0:T(8,128)(2,1)S(1)}, u32[]{:S(2)}) copy-start(bf16[32,1536]{1,0:T(8,128)(2,1)S(1)} %slice.605) | copy-start | bytes 294916
  398.3 36.9 %copy-start.191 = (bf16[8,1536]{1,0:T(8,128)(2,1)}, bf16[8,1536]{1,0:T(8,128)(2,1)S(1)}, u32[]{:S(2)}) copy-start(bf16[8,1536]{1,0:T(8,128)(2,1)S(1)} %slice.607) | copy-start | bytes 73732
  398.8 34.8 %collective-permute-start.1 = (bf16[496,1536]{1,0:T(8,128)(2,1)S(1)}, bf16[496,1536]{1,0:T(8,128)(2,1)S(1)}, u32[]{:S(2)}, u32[]{:S(2)}) collective-permute-start(bf16[496,1536]{1,0:T(8,128)(2,1)S(1)} %get-tuple-element.177), channel_id=1, source_target_pairs={{0,4},{2,6},{4,0},{6,2},{8,12},{10,14},{12,8},{14,10},{16,20},{18,... | collective-permute-start | bytes 4571144 | tf_op jit(solution)/shard_map/ppermute | solution.py:42
  436.6 89.3 %copy-start.189 = (f32[19,768]{1,0:T(8,128)S(1)}, f32[19,768]{1,0:T(8,128)}, u32[]{:S(2)}) copy-start(f32[19,768]{1,0:T(8,128)} %param.178) | copy-start | bytes 175108
  436.6 89.3 %copy-start.296 = (pred[2,16]{1,0:T(4,128)(4,1)S(1)}, pred[2,16]{1,0:T(4,128)(4,1)}, u32[]{:S(2)}) copy-start(pred[2,16]{1,0:T(4,128)(4,1)} %constant.328) | copy-start | bytes 100
  436.6 90.9 %copy-start.292 = (pred[4,16]{1,0:T(4,128)(4,1)S(1)}, pred[4,16]{1,0:T(4,128)(4,1)}, u32[]{:S(2)}) copy-start(pred[4,16]{1,0:T(4,128)(4,1)} %constant.329) | copy-start | bytes 196
  436.6 91.6 %copy-start.245 = (pred[16,16]{1,0:T(8,128)(4,1)S(1)}, pred[16,16]{1,0:T(8,128)(4,1)}, u32[]{:S(2)}) copy-start(pred[16,16]{1,0:T(8,128)(4,1)} %constant.331) | copy-start | bytes 772
  436.6 92.3 %copy-start.258 = (pred[8,16]{1,0:T(8,128)(4,1)S(1)}, pred[8,16]{1,0:T(8,128)(4,1)}, u32[]{:S(2)}) copy-start(pred[8,16]{1,0:T(8,128)(4,1)} %constant.330) | copy-start | bytes 388
  437.3 95.0 %slice-start.7 = ((f32[19,768]{1,0:T(8,128)}), f32[4,768]{1,0:T(4,128)S(1)}, s32[]{:S(2)}) async-start(f32[19,768]{1,0:T(8,128)} %param.178), calls=%async_computation.13 | async-start | bytes 24576 | tf_op jit(solution)/shard_map/slice | solution.py:345
  437.3 102.5 %copy-start.269 = (s32[3]{0:T(128)S(1)}, s32[3]{0:T(128)}, u32[]{:S(2)}) copy-start(s32[3]{0:T(128)} %copy-done.268) | copy-start | bytes 40
  437.3 103.9 %copy-start.323 = (s32[256]{0:T(256)S(1)}, s32[256]{0:T(256)}, u32[]{:S(2)}) copy-start(s32[256]{0:T(256)} %iota_multiply_fusion.2) | copy-start | bytes 3076
  437.3 104.7 %copy-start.329 = (s32[128]{0:T(128)S(1)}, s32[128]{0:T(128)}, u32[]{:S(2)}) copy-start(s32[128]{0:T(128)} %iota_multiply_fusion.3) | copy-start | bytes 1540
  437.3 104.7 %copy-start.330 = (s32[16]{0:T(128)S(1)}, s32[16]{0:T(128)}, u32[]{:S(2)}) copy-start(s32[16]{0:T(128)} %iota_add_fusion.2) | copy-start | bytes 196
  438.3 104.4 %copy-start.306 = (s32[512]{0:T(512)S(1)}, s32[512]{0:T(512)}, u32[]{:S(2)}) copy-start(s32[512]{0:T(512)} %iota_multiply_fusion.1) | copy-start | bytes 6148
  439.1 86.8 %copy-start.158 = (bf16[16,1536]{1,0:T(8,128)(2,1)}, bf16[16,1536]{1,0:T(8,128)(2,1)S(1)}, u32[]{:S(2)}) copy-start(bf16[16,1536]{1,0:T(8,128)(2,1)S(1)} %slice.612) | copy-start | bytes 147460
  439.8 167.3 %collective-permute-start.2 = (bf16[992,1536]{1,0:T(8,128)(2,1)}, bf16[992,1536]{1,0:T(8,128)(2,1)}, u32[]{:S(2)}, u32[]{:S(2)}) collective-permute-start(bf16[992,1536]{1,0:T(8,128)(2,1)} %get-tuple-element.169), channel_id=1, source_target_pairs={{0,8},{2,10},{4,12},{6,14},{8,0},{10,2},{12,4},{14,6},{16,24},{18,... | collective-permute-start | bytes 9142280 | tf_op jit(solution)/shard_map/ppermute | solution.py:42
  542.7 95.8 %copy-start.271 = (s32[128,16]{0,1:T(8,128)}, s32[128,16]{0,1:T(8,128)S(1)}, u32[]{:S(2)}) copy-start(s32[128,16]{0,1:T(8,128)S(1)} %get-tuple-element.129) | copy-start | bytes 24580
  574.7 12.0 copy-start.142
  574.7 12.9 copy-start.157
  614.0 129.4 %collective-permute-start.3 = (bf16[960,1536]{1,0:T(8,128)(2,1)}, bf16[960,1536]{1,0:T(8,128)(2,1)}, u32[]{:S(2)}, u32[]{:S(2)}) collective-permute-start(bf16[960,1536]{1,0:T(8,128)(2,1)} %pad_maximum_fusion.4), channel_id=1, source_target_pairs={{0,16},{2,18},{4,20},{6,22},{8,24},{10,26},{12,28},{14,30},{16,0},... | collective-permute-start | bytes 8847368 | tf_op jit(solution)/shard_map/ppermute | solution.py:42
  638.5 106.1 %copy-start.119 = (bf16[1,64,2,16,48]{1,4,3,2,0:T(8,128)(2,1)S(1)}, bf16[1,64,2,16,48]{1,4,3,2,0:T(8,128)(2,1)}, u32[]{:S(2)}) copy-start(bf16[1,64,2,16,48]{1,4,3,2,0:T(8,128)(2,1)} %fusion.273) | copy-start | bytes 589828
  641.8 104.0 %copy-start.236 = (f32[16,128]{1,0:T(8,128)}, f32[16,128]{1,0:T(8,128)S(1)}, u32[]{:S(2)}) copy-start(f32[16,128]{1,0:T(8,128)S(1)} %exponential_reduce_fusion) | copy-start | bytes 24580
  641.8 103.2 %copy-start.231 = (bf16[16,8,48]{2,1,0:T(8,128)(2,1)S(1)}, bf16[16,8,48]{2,1,0:T(8,128)(2,1)}, u32[]{:S(2)}) copy-start(bf16[16,8,48]{2,1,0:T(8,128)(2,1)} %gather_fusion.14) | copy-start | bytes 36868
  641.8 103.2 %copy-start.307 = (s32[16,8]{1,0:T(8,128)S(1)}, s32[16,8]{1,0:T(8,128)}, u32[]{:S(2)}) copy-start(s32[16,8]{1,0:T(8,128)} %copy.1628) | copy-start | bytes 1540
  641.9 103.2 %copy-start.310 = (s32[128,16]{0,1:T(8,128)S(1)}, s32[128,16]{0,1:T(8,128)}, u32[]{:S(2)}) copy-start(s32[128,16]{0,1:T(8,128)} %get-tuple-element.128) | copy-start | bytes 24580
  765.1 60.0 %copy-start.5 = (bf16[1,1024,2,16,48]{1,4,3,2,0:T(8,128)(2,1)}, bf16[1,1024,2,16,48]{1,4,3,2,0:T(8,128)(2,1)S(1)}, u32[]{:S(2)}) copy-start(bf16[1,1024,2,16,48]{1,4,3,2,0:T(8,128)(2,1)S(1)} %maximum_select_fusion.1) | copy-start | bytes 9437188
  768.4 27.4 %copy-start.196 = (f32[64,16]{0,1:T(8,128)}, f32[64,16]{0,1:T(8,128)S(1)}, u32[]{:S(2)}) copy-start(f32[64,16]{0,1:T(8,128)S(1)} %fusion.413) | copy-start | bytes 12292
  800.1 13.2 copy-start.240
  863.5 20.1 copy-start.25
  863.5 20.1 copy-start.301
  863.7 19.9 copy-start.313
  1002.5 12.7 copy-start.4
  1050.1 129.0 %collective-permute-start.4 = (bf16[960,1536]{1,0:T(8,128)(2,1)}, bf16[960,1536]{1,0:T(8,128)(2,1)}, u32[]{:S(2)}, u32[]{:S(2)}) collective-permute-start(bf16[960,1536]{1,0:T(8,128)(2,1)} %pad_maximum_fusion.5), channel_id=1, source_target_pairs={{0,16},{2,18},{4,20},{6,22},{8,24},{10,26},{12,28},{14,30},{16,0},... | collective-permute-start | bytes 8847368 | tf_op jit(solution)/shard_map/ppermute | solution.py:42
  1085.7 20.0 copy-start.276
  1115.5 63.6 %copy-start.10 = (f32[512,1536]{1,0:T(8,128)S(1)}, f32[512,1536]{1,0:T(8,128)}, u32[]{:S(2)}) copy-start(f32[512,1536]{1,0:T(8,128)} %copy.1815) | copy-start | bytes 9437188
  1189.8 68.2 %collective-permute-start.5 = (bf16[992,1536]{1,0:T(8,128)(2,1)}, bf16[992,1536]{1,0:T(8,128)(2,1)}, u32[]{:S(2)}, u32[]{:S(2)}) collective-permute-start(bf16[992,1536]{1,0:T(8,128)(2,1)} %fusion.325), channel_id=1, source_target_pairs={{0,8},{2,10},{4,12},{6,14},{8,0},{10,2},{12,4},{14,6},{16,24},{18,... | collective-permute-start | bytes 9142280 | tf_op jit(solution)/shard_map/ppermute | solution.py:42
  1270.0 35.3 %collective-permute-start.6 = (bf16[496,1536]{1,0:T(8,128)(2,1)}, bf16[496,1536]{1,0:T(8,128)(2,1)}, u32[]{:S(2)}, u32[]{:S(2)}) collective-permute-start(bf16[496,1536]{1,0:T(8,128)(2,1)} %constant_dynamic-update-slice_fusion.22), channel_id=1, source_target_pairs={{0,4},{2,6},{4,0},{6,2},{8,12},{10,14},{12,8},{14,10},{16,20},{18,... | collective-permute-start | bytes 4571144 | tf_op jit(solution)/shard_map/ppermute | solution.py:42
  1317.5 47.1 %collective-permute-start.7 = (bf16[248,1536]{1,0:T(8,128)(2,1)}, bf16[248,1536]{1,0:T(8,128)(2,1)}, u32[]{:S(2)}, u32[]{:S(2)}) collective-permute-start(bf16[248,1536]{1,0:T(8,128)(2,1)} %constant_dynamic-update-slice_fusion.23), channel_id=1, source_target_pairs={{0,2},{2,0},{4,6},{6,4},{8,10},{10,8},{12,14},{14,12},{16,18},{18,... | collective-permute-start | bytes 2285576 | tf_op jit(solution)/shard_map/ppermute | solution.py:42
  1395.9 498.7 %reduce-scatter.3.cloned.1.call-start = ((), (), s32[]{:S(2)}) async-start(), calls=%async_computation.4 | async-start | bytes 38928384 | tf_op jit(solution)/shard_map/reduce_scatter | solution.py:520
  1416.7 12.2 copy-start.83
  1549.4 391.4 %copy-start.131 = (f32[48,2,768]{2,1,0:T(2,128)S(1)}, f32[48,2,768]{2,1,0:T(2,128)}, u32[]{:S(2)}) copy-start(f32[48,2,768]{2,1,0:T(2,128)} %param.175) | copy-start | bytes 884740
  1549.4 391.4 %copy-start.169 = (f32[48,2,768]{2,1,0:T(2,128)S(1)}, f32[48,2,768]{2,1,0:T(2,128)}, u32[]{:S(2)}) copy-start(f32[48,2,768]{2,1,0:T(2,128)} %param.177) | copy-start | bytes 884740
  1549.4 391.4 %copy-start.170 = (f32[48,2,768]{2,1,0:T(2,128)S(1)}, f32[48,2,768]{2,1,0:T(2,128)}, u32[]{:S(2)}) copy-start(f32[48,2,768]{2,1,0:T(2,128)} %param.176) | copy-start | bytes 884740
  1549.9 390.9 %copy-start.132 = (f32[48,2,768]{2,0,1:T(8,128)S(1)}, f32[48,2,768]{2,0,1:T(8,128)}, u32[]{:S(2)}) copy-start(f32[48,2,768]{2,0,1:T(8,128)} %reduce-scatter.5.cloned.1.call-done) | copy-start | bytes 884740
  1944.3 63.4 %copy-start.2 = (f32[24,96,96]{2,1,0:T(8,128)}, f32[24,96,96]{2,1,0:T(8,128)S(1)}, u32[]{:S(2)}) copy-start(f32[24,96,96]{2,1,0:T(8,128)S(1)} %broadcast_multiply_fusion) | copy-start | bytes 2654212
  1946.9 52.0 %copy-start.3 = (f32[24,96,96]{2,1,0:T(8,128)}, f32[24,96,96]{2,1,0:T(8,128)S(1)}, u32[]{:S(2)}) copy-start(f32[24,96,96]{2,1,0:T(8,128)S(1)} %fusion.73) | copy-start | bytes 2654212
  1949.5 21.1 %copy-start.8 = (f32[24,96,96]{2,1,0:T(8,128)}, f32[24,96,96]{2,1,0:T(8,128)S(1)}, u32[]{:S(2)}) copy-start(f32[24,96,96]{2,1,0:T(8,128)S(1)} %get-tuple-element.262) | copy-start | bytes 2654212
  (295 other events, 1065.9 us)
Sparse Core Ops, SparseCore 0:
  11.6 66.3 all-gather.2
  81.4 123.4 all-gather.4
  1396.1 133.6 reduce-scatter.4
  1546.2 348.3 reduce-scatter.2
where the time goes:
time: 2040 us; the launch traced here: 2020 us
  waiting for transfers between devices  822 us (40%)
  local copies, waits for them, and re-layouts  562 us (28%)
  matrix products  253 us (12%)
  other arithmetic  225 us (11%)
  blocking collectives  127 us (6%)
  between operations  22.8 us (1%)
    reduce_scatter x1, waiting for transfers between devices, per_device(): lax.psum_scatter(slot_grads, ('seq', 'opt'), scatter_dimension=0, tiled=T...  343 us
    ppermute x8, waiting for transfers between devices, from_partner(): return lax.ppermute(value, axis, pairs)  290 us
    all_gather x1, waiting for transfers between devices, per_device(): lax.all_gather(layer_blocks.astype(jnp.bfloat16), ('seq', 'opt'), axis=0,...  124 us
    scatter x1, local copies, waits for them, and re-layouts, per_device(): natural = jnp.zeros_like(all_blocks).at[owners].set(all_blocks)  104 us
    psum x1, blocking collectives, per_device(): lax.psum(jnp.sum(tile_mask.astype(jnp.float32)), ('seq', 'opt'))  85.9 us
    broadcast_in_dim x103, local copies, waits for them, and re-layouts, spread_rows(): spread_out = jnp.where(hit_mask, values[:, None], filler)  69.9 us
    all_gather x1, waiting for transfers between devices, per_device(): lax.all_gather(io_weights.astype(jnp.bfloat16), ('seq', 'opt'), axis=0, t...  64.1 us
    another operation x2, local copies, waits for them, and re-layouts, disassemble(): upper_mats.reshape(LAYERS, D // BLOCK, BLOCK, col_count, BLOCK)  48.9 us
  transfers between devices with their start and end apart: 12, of which 9 were waited for; matrix products, arithmetic and copies ran while one was open for 20% of the time, Pallas kernels for 0%

commit v1 on v0

--- a/solution.py
+++ b/solution.py
@@ -5,6 +5,8 @@
 import jax.numpy as jnp
 import numpy as np
 from jax import lax
+from jax.experimental import pallas as pl
+from jax.experimental.pallas import tpu as pltpu
 from jax.sharding import PartitionSpec as P
 
 D = 768
@@ -557,9 +559,692 @@
     )
 
 
+LANES=4*BLOCK
+
+def swap(value, axis, mask):
+    return lax.ppermute(value, axis, [(s, s ^ mask) for s in range(lax.axis_size(axis))])
+
+def tree_pieces(own, bits):
+    rows = own.shape[0]; half = rows // 2
+    far = [own]
+    if bits > 2:
+        far.append(swap(own, "seq", 4))
+    if bits > 3:
+        far.append(swap(own, "seq", 8))
+        far.append(swap(far[2], "seq", 4))
+    out = []
+    for piece in far:
+        first, second = piece[:half], piece[half:]
+        first_x = swap(first, "seq", 1)
+        second_y = swap(second, "seq", 2)
+        first_y = swap(jnp.concatenate([first, first_x]), "seq", 2)
+        second_x = swap(jnp.concatenate([second, second_y]), "seq", 1)
+        out.append(jnp.concatenate([piece, first_x, second_y, first_y, second_x]))
+    return out
+
+IO=48
+def assemble_kernel(n_buf, index_ref, io_ref, *refs):
+    bufs = refs[:n_buf]
+    upper_ref, lower_ref, win_ref, whead_ref = refs[n_buf:n_buf+4]
+    held, blocks, stage, in_sem, out_sem, io_sem = refs[n_buf+4:]
+    rows = bufs[0].shape[0]
+    groups = blocks.shape[0] // 4 // n_buf // 8
+    half = rows // 8
+    loads = [pltpu.make_async_copy(b, held.at[pl.ds(k*rows, rows)], in_sem.at[k]) for k, b in enumerate(bufs)]
+    for c in loads: c.start()
+    for k, c in enumerate(loads):
+        c.wait()
+        def unpack(u, carry, k=k):
+            base = k*rows + u*half
+            for g in range(groups):
+                packed = held[pl.ds(pl.multiple_of(base + g*BLOCK, 48), BLOCK), :]
+                for t in range(4):
+                    blocks[(k*8+u)*groups*4 + g*4 + t, :, :BLOCK] = packed[:, BLOCK*t:BLOCK*(t+1)]
+            return carry
+        lax.fori_loop(0, 8, unpack, 0)
+    n_dev = io_ref.shape[1]
+    def io_copy(d, carry):
+        for m, out in ((0, win_ref), (1, whead_ref)):
+            off = pl.multiple_of(io_ref[m, d], IO)
+            for h in range(2):
+                pltpu.make_async_copy(held.at[pl.ds(off + h*IO, IO)],
+                    out.at[pl.ds(pl.multiple_of(d*IO, IO), IO), pl.ds(h*LANES, LANES)], io_sem.at[m]).start()
+        return carry
+    lax.fori_loop(0, n_dev, io_copy, 0)
+    outs=[]
+    def chunk(index, out, first):
+        slot = index % 2
+        if index >= 2: outs[index-2].wait()
+        st = stage.at[slot]
+        def one(c, carry):
+            n0 = first(c)
+            st[:, pl.ds(pl.multiple_of(c*LANES, 128), LANES)] = jnp.concatenate([blocks[index_ref[n0+t], :, :BLOCK] for t in range(4)], axis=1)
+            return carry
+        lax.fori_loop(0, U, one, 0, unroll=2)
+        c = out(st, out_sem.at[slot]); c.start(); outs.append(c)
+    U = (4*D+FF)//LANES
+    for i in range(D//BLOCK):
+        chunk(i, lambda st, sem, i=i: pltpu.make_async_copy(st, upper_ref.at[pl.ds(i*BLOCK, BLOCK)], sem), lambda c, i=i: i*4*U+4*c)
+    base = D//BLOCK*4*U
+    per = U//2
+    for j in range(FF//BLOCK//per):
+        def out(st, sem, j=j):
+            return Multi([pltpu.make_async_copy(st.at[:, pl.ds(b*D, D)], lower_ref.at[pl.ds((j*per+b)*BLOCK, BLOCK)], sem) for b in range(per)])
+        chunk(D//BLOCK+j, out, lambda c, j=j: base + (j*per*2+c)*4)
+    outs[-2].wait(); outs[-1].wait()
+    for m, out in ((0, win_ref), (1, whead_ref)):
+        pltpu.make_async_copy(out, out, io_sem.at[m]).wait()
+class Multi:
+    def __init__(s, cs): s.cs=cs
+    def start(s):
+        for c in s.cs: c.start()
+    def wait(s):
+        for c in s.cs: c.wait()
+
+def join_weights(bufs, index, io_off):
+    n=len(bufs); total=sum(b.shape[0] for b in bufs)
+    return pl.pallas_call(partial(assemble_kernel, n),
+        out_shape=[jax.ShapeDtypeStruct(s, jnp.bfloat16) for s in ((D,4*D+FF),(FF,D),(FEAT,D),(FEAT,D))],
+        in_specs=[pl.BlockSpec(memory_space=pltpu.SMEM)]*2+[pl.BlockSpec(memory_space=pl.ANY)]*n,
+        out_specs=[pl.BlockSpec(memory_space=pl.ANY)]*4,
+        scratch_shapes=[pltpu.VMEM((total,LANES),jnp.bfloat16), pltpu.VMEM((768,BLOCK,128),jnp.bfloat16), pltpu.VMEM((2,BLOCK,4*D+FF),jnp.bfloat16),
+            pltpu.SemaphoreType.DMA((n,)), pltpu.SemaphoreType.DMA((2,)), pltpu.SemaphoreType.DMA((2,))],
+        compiler_params=pltpu.CompilerParams(vmem_limit_bytes=56<<20),
+        name="join_weights",
+    )(index, io_off, *bufs)
+
+def pack_blocks(blocks):
+    g=blocks.shape[0]//4
+    return blocks.reshape(g,4,BLOCK,BLOCK).transpose(0,2,1,3).reshape(g*BLOCK,LANES)
+def fold(rows):
+    return jnp.concatenate([rows[:,:LANES],rows[:,LANES:]],axis=0)
+def pack_shard(blocks, io):
+    b=pack_blocks(blocks.astype(jnp.bfloat16)); h=b.shape[0]//2; io=io.astype(jnp.bfloat16)
+    return jnp.concatenate([b[:h],fold(io[:,0]),b[h:],fold(io[:,1])],axis=0)
+def offsets(owners, seq_index, core, n_slots):
+    gh=n_slots//8; half=gh*BLOCK+2*IO
+    def unit(rel, ro, h):
+        xy=rel%4
+        both=jnp.where(xy==0,h,jnp.where(h==0,jnp.where(xy==1,2,xy+2),jnp.where(xy==2,3,jnp.where(xy==1,6,7))))
+        return (rel//4+4*ro)*8+both
+    slot=jnp.arange(768,dtype=jnp.int32)
+    d=slot//n_slots; s=slot%n_slots
+    u=unit((d//2)^seq_index,(d%2)^core,s//4//gh)
+    index=jnp.zeros((768,),jnp.int32).at[owners].set((u*gh+s//4%gh)*4+s%4, unique_indices=True, mode="promise_in_bounds")
+    dev=jnp.arange(32,dtype=jnp.int32)
+    io=jnp.stack([unit((dev//2)^seq_index,(dev%2)^core,h)*half+gh*BLOCK for h in (0,1)])
+    return index, io.astype(jnp.int32)
+def gather_weights(layer_blocks, io_weights, owners):
+    si=lax.axis_index("seq"); ci=lax.axis_index("opt")
+    ps=tree_pieces(pack_shard(layer_blocks,io_weights),4)
+    os=[swap(p,"opt",1) for p in ps]
+    index,io=offsets(owners,si,ci,layer_blocks.shape[0])
+    return join_weights(ps+os,index,io)
+
+HD=48; HEADS=16; SLIDES=4; SEG=1024; N=2048; H=512; TQ=256; TK=128
+C2=HD**-0.5*math.log2(math.e)
+def place_facts(index, head, lengths_ref, core):
+    parity=lax.rem(head+(index//H)%2,2)
+    pos=(index//SEG)*SEG+2*(index%H)+parity
+    slide=jnp.zeros_like(index); end=jnp.int32(0)
+    for i in range(SLIDES-1):
+        end=end+lengths_ref[core,i]
+        slide=slide+jnp.where(pos>=end,1,0)
+    d=(pos-head)&15
+    level=sum(jnp.where((d&(2**i-1))==0,1,0) for i in range(1,5))
+    return slide.astype(jnp.float32), level.astype(jnp.float32)
+
+def arrange(src, dst, odd):
+    for pair in range(8):
+        first, second = src[2*pair], src[2*pair+1]
+        turn=lambda t: jnp.concatenate([t[:,64:],t[:,:64]],axis=1)
+        ft, st = turn(first), turn(second)
+        low=lax.broadcasted_iota(jnp.int32,first.shape,1)<64
+        evens=jnp.where(low,first,st); odds=jnp.where(low,ft,second)
+        near=jnp.where(odd,odds,evens); far=jnp.where(odd,evens,odds)
+        at=(pair//4)*SEG+(pair%4)*128
+        dst[:,at:at+128]=near.astype(dst.dtype); dst[:,at+H:at+H+128]=far.astype(dst.dtype)
+
+def restore(get, put, odd):
+    for pair in range(8):
+        at=(pair//4)*SEG+(pair%4)*128
+        near, far = get(at), get(at+H)
+        evens=jnp.where(odd,far,near); odds=jnp.where(odd,near,far)
+        turn=lambda t: jnp.concatenate([t[:,64:],t[:,:64]],axis=1)
+        low=lax.broadcasted_iota(jnp.int32,evens.shape,1)<64
+        put(2*pair, jnp.where(low,evens,turn(odds)))
+        put(2*pair+1, jnp.where(low,turn(evens),odds))
+
+def setup(lengths_ref, ids_ref, slide_k, level_k, row_facts):
+    head, core = ids_ref[0], ids_ref[1]
+    def fill(i, c):
+        idx=lax.broadcasted_iota(jnp.int32,(TK,128),0)+i*TK
+        s,l=place_facts(idx,head,lengths_ref,core)
+        slide_k[pl.ds(pl.multiple_of(i*TK,TK),TK),:]=s
+        level_k[pl.ds(pl.multiple_of(i*TK,TK),TK),:]=l
+        return c
+    lax.fori_loop(0,N//TK,fill,0)
+    idx=lax.broadcasted_iota(jnp.int32,(8,N),1)
+    s,l=place_facts(idx,head,lengths_ref,core)
+    row_facts[0:8,:]=s; row_facts[8:16,:]=l
+
+def key_rows(seg, near):
+    own=[(seg*SEG+i*TK,True) for i in range(SEG//TK)]
+    other=[((1-seg)*SEG+i*TK,False) for i in range(H//TK)] if near else []
+    return own+other
+
+def wide(x): return jnp.concatenate([x]*(TQ//128),axis=1)
+
+def forward_kernel(lengths_ref, ids_ref, qkv_ref, o_ref, out_ref, lse_ref, qkvT, krow, slide_k, level_k, row_facts, s_ref, p_ref):
+    odd=lax.rem(ids_ref[0],2)==1
+    arrange(qkv_ref, qkvT, odd)
+    setup(lengths_ref, ids_ref, slide_k, level_k, row_facts)
+    for i in range(N//128):
+        krow[i*128:(i+1)*128,:]=qkvT[HD:2*HD,i*128:(i+1)*128].astype(jnp.float32).T.astype(jnp.bfloat16)
+    for seg in range(2):
+        for near in (True,False):
+            tiles=key_rows(seg,near)
+            def part(c, carry, seg=seg, near=near, tiles=tiles):
+                at=pl.multiple_of(seg*SEG+(0 if near else H)+c*TQ,TQ)
+                qT=qkvT[0:HD,pl.ds(at,TQ)]
+                sq=row_facts[0:1,pl.ds(at,TQ)]; lq=row_facts[8:9,pl.ds(at,TQ)]
+                top=jnp.full((8,TQ),-jnp.inf,jnp.float32)
+                for t,(r,own) in enumerate(tiles):
+                    s=jnp.dot(krow[r:r+TK,:],qT,preferred_element_type=jnp.float32)
+                    s=jnp.where(wide(slide_k[r:r+TK,:])==sq,s,-1e30)
+                    s_ref[t*TK:(t+1)*TK,:]=s
+                    top=jnp.maximum(top,jnp.max(s.reshape(TK//8,8,TQ),axis=0))
+                m=jnp.max(top,axis=0,keepdims=True)
+                total=jnp.zeros((8,TQ),jnp.float32)
+                for t,(r,own) in enumerate(tiles):
+                    e=jnp.exp2((s_ref[t*TK:(t+1)*TK,:]-m)*C2)
+                    if near:
+                        lk=wide(level_k[r:r+TK,:])
+                        e=e*(jnp.minimum(lk,lq)+1.0 if own else jnp.minimum(lk,lq))
+                    total=total+jnp.sum(e.reshape(TK//8,8,TQ),axis=0)
+                    p_ref[t*TK:(t+1)*TK,:]=e.astype(jnp.bfloat16)
+                l=jnp.sum(total,axis=0,keepdims=True)
+                acc=jnp.zeros((HD,TQ),jnp.float32)
+                acc=jnp.dot(qkvT[2*HD:3*HD,seg*SEG:(seg+1)*SEG],p_ref[0:SEG,:],preferred_element_type=jnp.float32)
+                if near:
+                    acc=acc+jnp.dot(qkvT[2*HD:3*HD,(1-seg)*SEG:(1-seg)*SEG+H],p_ref[SEG:SEG+H,:],preferred_element_type=jnp.float32)
+                o_ref[:,pl.ds(at,TQ)]=acc/l
+                lse_ref[:,pl.ds(at,TQ)]=jnp.broadcast_to(m*C2+jnp.log2(l),(8,TQ))
+                return carry
+            lax.fori_loop(0,H//TQ,part,0)
+    def put(c,v): out_ref[c]=v.astype(jnp.bfloat16)
+    restore(lambda at: o_ref[:,at:at+128], put, odd)
+
+def backward_kernel(lengths_ref, ids_ref, qkv_ref, do_ref, o_ref, lse_ref, out_ref, qkvT, doT, rows, slide_k, level_k, row_facts, dqT, dkv, p_ref, ds_ref):
+    odd=lax.rem(ids_ref[0],2)==1
+    arrange(qkv_ref, qkvT, odd)
+    arrange(do_ref, doT, odd)
+    setup(lengths_ref, ids_ref, slide_k, level_k, row_facts)
+    for i in range(N//128):
+        l=slice(i*128,(i+1)*128)
+        for j in range(3):
+            rows[j,l,:]=qkvT[j*HD:(j+1)*HD,l].astype(jnp.float32).T.astype(jnp.bfloat16)
+        rows[3,l,:]=doT[:,l].astype(jnp.float32).T.astype(jnp.bfloat16)
+    dkv[...]=jnp.zeros_like(dkv)
+    for seg in range(2):
+        for near in (True,False):
+            tiles=key_rows(seg,near)
+            def part(c, carry, seg=seg, near=near, tiles=tiles):
+                at=pl.multiple_of(seg*SEG+(0 if near else H)+c*TQ,TQ)
+                qT=qkvT[0:HD,pl.ds(at,TQ)]; gT=doT[:,pl.ds(at,TQ)]
+                q=rows[0,pl.ds(at,TQ),:]; g=rows[3,pl.ds(at,TQ),:]
+                sq=row_facts[0:1,pl.ds(at,TQ)]; lq=row_facts[8:9,pl.ds(at,TQ)]
+                lse=lse_ref[0:1,pl.ds(at,TQ)]
+                inner=jnp.sum(gT.astype(jnp.float32)*o_ref[:,pl.ds(at,TQ)],axis=0,keepdims=True)
+                for t,(r,own) in enumerate(tiles):
+                    s=jnp.dot(rows[1,r:r+TK,:],qT,preferred_element_type=jnp.float32)
+                    dp=jnp.dot(rows[2,r:r+TK,:],gT,preferred_element_type=jnp.float32)
+                    e=jnp.exp2(s*C2-lse)
+                    if near:
+                        lk=wide(level_k[r:r+TK,:])
+                        e=e*(jnp.minimum(lk,lq)+1.0 if own else jnp.minimum(lk,lq))
+                    e=jnp.where(wide(slide_k[r:r+TK,:])==sq,e,0.0)
+                    p_ref[t*TK:(t+1)*TK,:]=e.astype(jnp.bfloat16)
+                    ds_ref[t*TK:(t+1)*TK,:]=(e*(dp-inner)).astype(jnp.bfloat16)
+                dq=jnp.dot(qkvT[HD:2*HD,seg*SEG:(seg+1)*SEG],ds_ref[0:SEG,:],preferred_element_type=jnp.float32)
+                if near:
+                    dq=dq+jnp.dot(qkvT[HD:2*HD,(1-seg)*SEG:(1-seg)*SEG+H],ds_ref[SEG:SEG+H,:],preferred_element_type=jnp.float32)
+                dqT[:,pl.ds(at,TQ)]=dq*HD**-0.5
+                own=slice(seg*SEG,(seg+1)*SEG)
+                dkv[0,own,:]+=jnp.dot(ds_ref[0:SEG,:],q,preferred_element_type=jnp.float32)
+                dkv[1,own,:]+=jnp.dot(p_ref[0:SEG,:],g,preferred_element_type=jnp.float32)
+                if near:
+                    oth=slice((1-seg)*SEG,(1-seg)*SEG+H)
+                    dkv[0,oth,:]+=jnp.dot(ds_ref[SEG:SEG+H,:],q,preferred_element_type=jnp.float32)
+                    dkv[1,oth,:]+=jnp.dot(p_ref[SEG:SEG+H,:],g,preferred_element_type=jnp.float32)
+                return carry
+            lax.fori_loop(0,H//TQ,part,0)
+    def putter(j):
+        def put(c,v): out_ref[c,j*HD:(j+1)*HD,:]=v.astype(jnp.bfloat16)
+        return put
+    restore(lambda at: dqT[:,at:at+128], putter(0), odd)
+    restore(lambda at: dkv[0,at:at+128,:].T*HD**-0.5, putter(1), odd)
+    restore(lambda at: dkv[1,at:at+128,:].T, putter(2), odd)
+
+def vm(): return pl.BlockSpec(memory_space=pltpu.VMEM)
+def sm_(): return pl.BlockSpec(memory_space=pltpu.SMEM)
+F32=jnp.float32; BF=jnp.bfloat16
+def attend(lengths, ids, qkv):
+    return pl.pallas_call(forward_kernel,
+        out_shape=[jax.ShapeDtypeStruct((HD,N),F32),jax.ShapeDtypeStruct((16,HD,128),BF),jax.ShapeDtypeStruct((8,N),F32)],
+        in_specs=[sm_(),sm_(),vm()], out_specs=[vm()]*3,
+        scratch_shapes=[pltpu.VMEM((3*HD,N),BF),pltpu.VMEM((N,HD),BF),pltpu.VMEM((N,128),F32),pltpu.VMEM((N,128),F32),pltpu.VMEM((16,N),F32),
+            pltpu.VMEM((SEG+H,TQ),F32),pltpu.VMEM((SEG+H,TQ),BF)],
+        compiler_params=pltpu.CompilerParams(vmem_limit_bytes=48<<20), name="attend_forward")(lengths,ids,qkv)
+def attend_back(lengths, ids, qkv, do, o, lse):
+    return pl.pallas_call(backward_kernel,
+        out_shape=jax.ShapeDtypeStruct((16,3*HD,128),BF),
+        in_specs=[sm_(),sm_()]+[vm()]*4, out_specs=vm(),
+        scratch_shapes=[pltpu.VMEM((3*HD,N),BF),pltpu.VMEM((HD,N),BF),pltpu.VMEM((4,N,HD),BF),pltpu.VMEM((N,128),F32),pltpu.VMEM((N,128),F32),pltpu.VMEM((16,N),F32),
+            pltpu.VMEM((HD,N),F32),pltpu.VMEM((2,N,HD),F32),pltpu.VMEM((SEG+H,TQ),BF),pltpu.VMEM((SEG+H,TQ),BF)],
+        compiler_params=pltpu.CompilerParams(vmem_limit_bytes=48<<20), name="attend_backward")(lengths,ids,qkv,do,o,lse)
+
+I16=jnp.int16; F32=jnp.float32
+GROUP=48
+STEP_Q=32000.0
+def encode(x):
+    top=jnp.max(jnp.abs(x),axis=0,keepdims=True)
+    code=jnp.ceil(jnp.log2(jnp.maximum(top,1e-30))*256.0)
+    return x*(STEP_Q*jnp.exp2(code*(-1.0/256.0))), code
+def to16(v):
+    v=jnp.clip(jnp.round(v),-32767.0,32767.0)
+    return v.astype(jnp.int32).astype(I16)
+def scale_of(code16):
+    return jnp.exp2(code16.astype(jnp.int32).astype(F32)*(1.0/256.0))*(1.0/STEP_Q)
+
+def grads_kernel(index_ref, rel_ref, *refs):
+    (at_qkv,x_qkv,at_o,x_o,at_1,x_1,at_2,x_2,at_in,x_in,at_head,x_head)=refs[:12]
+    outs=refs[12:20]
+    slots, io, stage, sem = refs[20:]
+    def stripe(at_ref, x_ref, x_rows, i, c):
+        a=at_ref[pl.ds(pl.multiple_of(i*BLOCK,32),BLOCK),:]
+        if x_rows:
+            x=x_ref[pl.ds(pl.multiple_of(c*LANES,128),LANES),:]
+            return lax.dot_general(a,x,(((1,),(1,)),((),())),preferred_element_type=F32)
+        x=x_ref[:,pl.ds(pl.multiple_of(c*LANES,128),LANES)]
+        return jnp.dot(a,x,preferred_element_type=F32)
+    def place(w, n0):
+        parts=[encode(w[:GROUP]),encode(w[GROUP:])]
+        q=to16(jnp.concatenate([parts[0][0],parts[1][0]],axis=0))
+        codes=jnp.concatenate([parts[0][1],parts[1][1],jnp.zeros((14,LANES),F32)],axis=0)
+        codes=codes.astype(jnp.int32).astype(I16)
+        for t in range(4):
+            s=index_ref[n0+t]
+            slots[s,:BLOCK,:BLOCK]=q[:,BLOCK*t:BLOCK*(t+1)]
+            slots[s,BLOCK:,:BLOCK]=codes[:,BLOCK*t:BLOCK*(t+1)]
+    cols=(4*D+FF)//BLOCK
+    def run(at_ref,x_ref,x_rows,n_i,n_c,first):
+        def one(k,carry):
+            i=k//n_c; c=k%n_c
+            place(stripe(at_ref,x_ref,x_rows,i,c),first(i,c))
+            return carry
+        lax.fori_loop(0,n_i*n_c,one,0)
+    run(at_qkv,x_qkv,True,8,6,lambda i,c:i*cols+4*c)
+    run(at_o,x_o,False,8,2,lambda i,c:i*cols+24+4*c)
+    run(at_1,x_1,False,8,8,lambda i,c:i*cols+32+4*c)
+    run(at_2,x_2,False,32,2,lambda i,c:8*cols+i*8+4*c)
+    n_dev=rel_ref.shape[0]
+    def io_one(d,carry):
+        r=rel_ref[d]
+        for m,(at,x) in enumerate(((at_in,x_in),(at_head,x_head))):
+            w=jnp.dot(at[pl.ds(pl.multiple_of(d*IO,16),IO),:],x[...],preferred_element_type=F32)
+            q,code=encode(w); q=to16(q)
+            for h in range(2):
+                io[r,m,h*IO:(h+1)*IO,:]=q[:,h*LANES:(h+1)*LANES]
+            codes=jnp.concatenate([jnp.zeros((6,LANES),F32),code[:,:LANES],code[:,LANES:],jnp.zeros((8,LANES),F32)],axis=0)
+            io[r,m,2*IO:,:]=codes.astype(jnp.int32).astype(I16)
+        return carry
+    lax.fori_loop(0,n_dev,io_one,0)
+    half=3*BLOCK+2*IO
+    started=[]
+    for k,out in enumerate(outs):
+        def one(xy,carry,k=k,out=out):
+            slot=xy%2
+            r=k*4+xy
+            @pl.when(xy>=2)
+            def _():
+                pltpu.make_async_copy(stage.at[slot],out.at[xy],sem.at[slot]).wait()
+            for h in range(2):
+                codes=jnp.zeros((16,LANES),jnp.int32)
+                for g in range(3):
+                    tiles=[slots[(r*6+h*3+g)*4+t,:,:BLOCK] for t in range(4)]
+                    whole=jnp.concatenate(tiles,axis=1)
+                    stage[slot,h,g*BLOCK:(g+1)*BLOCK,:]=whole[:BLOCK]
+                    codes=codes+pltpu.roll(whole[BLOCK:].astype(jnp.int32),2*g,0)
+                stage[slot,h,3*BLOCK:half,:]=io[r,h,:2*IO,:]
+                codes=codes+io[r,h,2*IO:,:].astype(jnp.int32)
+                stage[slot,h,half:,:]=codes.astype(I16)
+            pltpu.make_async_copy(stage.at[slot],out.at[xy],sem.at[slot]).start()
+            return carry
+        lax.fori_loop(0,4,one,0)
+        for slot in range(2):
+            pltpu.make_async_copy(stage.at[slot],out.at[slot],sem.at[slot]).wait()
+
+ROWS=3*BLOCK+2*IO+16
+def weight_grads(index, rel, *operands):
+    return pl.pallas_call(grads_kernel,
+        out_shape=[jax.ShapeDtypeStruct((4,2,ROWS,LANES),I16)]*8,
+        in_specs=[pl.BlockSpec(memory_space=pltpu.SMEM)]*2+[pl.BlockSpec(memory_space=pltpu.VMEM)]*12,
+        out_specs=[pl.BlockSpec(memory_space=pl.ANY)]*8,
+        scratch_shapes=[pltpu.VMEM((768,BLOCK+16,128),I16),pltpu.VMEM((32,2,2*IO+16,LANES),I16),pltpu.VMEM((2,2,ROWS,LANES),I16),pltpu.SemaphoreType.DMA((2,))],
+        compiler_params=pltpu.CompilerParams(vmem_limit_bytes=56<<20), name="weight_grads")(index,rel,*operands)
+
+def add_rows(refs, at):
+    raise NotImplementedError
+def decoded_sum(views, k):
+    total=None
+    for v in views:
+        s=scale_of(v[ROWS-16:ROWS,:])[k:k+1,:]
+        x=v[k*GROUP:(k+1)*GROUP,:].astype(jnp.int32).astype(F32)*s
+        total=x if total is None else total+x
+    return total
+def add_codes(views, out):
+    codes=[]
+    scales=[scale_of(v[ROWS-16:ROWS,:]) for v in views]
+    for k in range(8):
+        total=None
+        for v,s in zip(views,scales):
+            x=v[k*GROUP:(k+1)*GROUP,:].astype(jnp.int32).astype(F32)*s[k:k+1,:]
+            total=x if total is None else total+x
+        q,code=encode(total)
+        out[k*GROUP:(k+1)*GROUP,:]=to16(q)
+        codes.append(code)
+    codes.append(jnp.zeros((8,LANES),F32))
+    out[ROWS-16:ROWS,:]=jnp.concatenate(codes,axis=0).astype(jnp.int32).astype(I16)
+
+class At:
+    def __init__(s,ref,*i): s.ref,s.i=ref,i
+    def __getitem__(s,k): return s.ref[(*s.i,*k)]
+    def __setitem__(s,k,v): s.ref[(*s.i,*k)]=v
+
+def split_kernel(mine, theirs, send_a, keep_a, send_b, keep_b):
+    for h,plan in ((0,((send_a,(2,3)),(keep_a,(0,1)))),(1,((send_b,(1,3)),(keep_b,(0,2))))):
+        for out,xys in plan:
+            for j,xy in enumerate(xys):
+                add_codes([At(mine,xy,h),At(theirs,xy,h)],At(out,j))
+def code_call(kernel, name, outs, *args):
+    return pl.pallas_call(kernel, out_shape=[jax.ShapeDtypeStruct(s,t) for s,t in outs],
+        in_specs=[pl.BlockSpec(memory_space=pltpu.VMEM)]*len(args), out_specs=[pl.BlockSpec(memory_space=pltpu.VMEM)]*len(outs),
+        compiler_params=pltpu.CompilerParams(vmem_limit_bytes=32<<20), name=name)(*args)
+def plane_kernel(keep_a, got_a, keep_b, got_b, send_a, stay_a, send_b, stay_b):
+    for keep,got,send,stay in ((keep_a,got_a,send_a,stay_a),(keep_b,got_b,send_b,stay_b)):
+        add_codes([At(keep,1),At(got,1)],At(send))
+        add_codes([At(keep,0),At(got,0)],At(stay))
+def line_kernel(*refs):
+    stay_a,got_a,stay_b,got_b=refs[:4]; more=refs[4:-1]; out=refs[-1]
+    for h,(stay,got) in enumerate(((stay_a,got_a),(stay_b,got_b))):
+        add_codes([At(stay),At(got)]+[At(m,h) for m in more],At(out,h))
+def final_kernel(*refs):
+    stay_a,got_a,stay_b,got_b=refs[:4]; more=refs[4:-3]; blocks,io_in,io_head=refs[-3:]
+    for h,(stay,got,io) in enumerate(((stay_a,got_a,io_in),(stay_b,got_b,io_head))):
+        views=[At(stay),At(got)]+[At(m,h) for m in more]
+        scales=[scale_of(v[ROWS-16:ROWS,:]) for v in views]
+        for k in range(8):
+            total=None
+            for v,s in zip(views,scales):
+                x=v[k*GROUP:(k+1)*GROUP,:].astype(jnp.int32).astype(F32)*s[k:k+1,:]
+                total=x if total is None else total+x
+            if k<6:
+                for t in range(4):
+                    blocks[(h*3+k//2)*4+t,(k%2)*GROUP:(k%2+1)*GROUP,:]=total[:,t*BLOCK:(t+1)*BLOCK]
+            else:
+                io[:,(k-6)*LANES:(k-5)*LANES]=total
+HALF=(ROWS,LANES)
+def reduce_tree(pieces):
+    mine,theirs=pieces[:4],pieces[4:]
+    got=[None]*4
+    for k in (3,2,1,0): got[k]=swap(theirs[k],"opt",1)
+    far={}
+    for k in (3,2,1,0):
+        send_a,keep_a,send_b,keep_b=code_call(split_kernel,"split_halves",[((2,)+HALF,I16)]*4,mine[k],got[k])
+        got_a=swap(send_a,"seq",2); got_b=swap(send_b,"seq",1)
+        send_a,stay_a,send_b,stay_b=code_call(plane_kernel,"add_plane",[(HALF,I16)]*4,keep_a,got_a,keep_b,got_b)
+        got_a=swap(send_a,"seq",1); got_b=swap(send_b,"seq",2)
+        if k==3:
+            far[3]=swap(code_call(line_kernel,"add_line",[((2,)+HALF,I16)],stay_a,got_a,stay_b,got_b)[0],"seq",4)
+        elif k==2:
+            far[2]=swap(code_call(line_kernel,"add_line",[((2,)+HALF,I16)],stay_a,got_a,stay_b,got_b,far[3])[0],"seq",8)
+        elif k==1:
+            far[1]=swap(code_call(line_kernel,"add_line",[((2,)+HALF,I16)],stay_a,got_a,stay_b,got_b)[0],"seq",4)
+        else:
+            return code_call(final_kernel,"add_final",[((24,BLOCK,BLOCK),F32),((IO,D),F32),((IO,D),F32)],stay_a,got_a,stay_b,got_b,far[1],far[2])
+def slot_index(owners, seq_index, core, n_slots):
+    slot=jnp.arange(768,dtype=jnp.int32); d=slot//n_slots
+    rel=((d//2)^seq_index)+16*((d%2)^core)
+    index=jnp.zeros((768,),jnp.int32).at[owners].set(rel*n_slots+slot%n_slots,unique_indices=True,mode="promise_in_bounds")
+    dev=jnp.arange(32,dtype=jnp.int32)
+    return index,(((dev//2)^seq_index)+16*((dev%2)^core)).astype(jnp.int32)
+
+
+def fits(mesh):
+    return mesh.shape["seq"] == 16 and mesh.shape["opt"] == 2
+
+
+def sum_everywhere(value):
+    value = value + swap(value, "opt", 1)
+    for bit in range((lax.axis_size("seq") - 1).bit_length()):
+        value = value + swap(value, "seq", 2**bit)
+    return value
+
+
+def sum_scalar(value):
+    return sum_everywhere(jnp.broadcast_to(value, (8, 128)))[0, 0]
+
+
+def to_heads(parts):
+    return lax.all_to_all(parts, "seq", 0, 0, tiled=True)
+
+
+def evens_first(rows):
+    return rows.reshape((rows.shape[0] // 2, 2) + rows.shape[1:]).swapaxes(0, 1).reshape(rows.shape)
+
+
+def shampoo_products(left, right):
+    return jnp.einsum("kij,kjl->kil", left, right, precision=lax.Precision.HIGH)
+
+
+def inverse_roots(matrices):
+    identity = jnp.eye(matrices.shape[-1], dtype=jnp.float32)
+    regular = matrices + root_eps * identity
+    frob_norm = jnp.sqrt(jnp.sum(regular * regular, axis=(1, 2), keepdims=True))
+    scaled = 2.5 / frob_norm
+    moving = regular * scaled
+    root_mat = None
+    for sweep_id in range(NEWTON):
+        factor = (5.0 * identity - moving) * 0.25
+        if root_mat is None:
+            root_mat = factor * jnp.sqrt(jnp.sqrt(scaled))
+        else:
+            root_mat = shampoo_products(root_mat, factor)
+        if sweep_id < NEWTON - 1:
+            square = shampoo_products(factor, factor)
+            moving = shampoo_products(shampoo_products(square, square), moving)
+    return root_mat
+
+
+def fast_device(
+    features,
+    tile_mask,
+    lengths,
+    owners,
+    layer_blocks,
+    stat_left,
+    stat_right,
+    io_weights,
+    io_first,
+    io_second,
+    vectors,
+    vec_first,
+    vec_second,
+):
+    tok_dev = features.shape[1]
+    seq_index = lax.axis_index("seq")
+    core_index = lax.axis_index("opt")
+    ids = jnp.stack([seq_index, core_index]).astype(jnp.int32)
+    low_targets = evens_first(features[0])
+    targets = low_targets.astype(jnp.float32)
+    chosen = evens_first(tile_mask[0])[:, None] > 0
+    lengths_row = lax.dynamic_index_in_dim(lengths, core_index, 0, keepdims=False)
+    places = seq_index * tok_dev + evens_first(jnp.arange(tok_dev, dtype=jnp.int32))
+    tile_count = sum_scalar(jnp.sum(tile_mask.astype(jnp.float32)))
+    upper, lower, in_weight, head_weight = gather_weights(layer_blocks, io_weights, owners)
+    layer_rows, tail_rows = unpack(vectors)
+    row_set = layer_rows[0]
+    token_vec = tail_rows[3 + FEAT // D :].reshape(FEAT)
+    head_bias = tail_rows[3 : 3 + FEAT // D].reshape(FEAT)
+    inputs = jnp.where(chosen, token_vec[None, :], targets).astype(jnp.bfloat16)
+    hidden = jnp.dot(inputs, in_weight, preferred_element_type=jnp.float32) + tail_rows[2][None, :]
+    hidden = hidden + sine_places(slide_offsets(lengths_row, places))
+
+    normed = layer_norm(hidden, row_set[0], row_set[1]).astype(jnp.bfloat16)
+    biases = jnp.concatenate([row_set[2], jnp.zeros_like(row_set[2]), row_set[3]])
+    qkv_weight = upper[:, : 3 * D]
+    out_weight = upper[:, 3 * D : 4 * D]
+    up_weight = upper[:, 4 * D :]
+    packed = lax.dot_general(
+        qkv_weight, normed, (((0,), (1,)), ((), ())), preferred_element_type=jnp.float32
+    )
+    packed = (packed + biases[:, None]).astype(jnp.bfloat16)
+    by_head = packed.reshape(3, HEADS, HEAD_DIM, tok_dev).swapaxes(0, 1)
+    own_head = to_heads(by_head.reshape(HEADS, 3 * HEAD_DIM, tok_dev))
+    head_out, mixed_parts, head_totals = attend(lengths, ids, own_head)
+    mixed_low = to_heads(mixed_parts).reshape(D, tok_dev)
+    middle = hidden + contract_rows(mixed_low, out_weight) + row_set[4][None, :]
+    second = layer_norm(middle, row_set[5], row_set[6]).astype(jnp.bfloat16)
+    before = (
+        jnp.dot(second, up_weight, preferred_element_type=jnp.float32)
+        + row_set[8:].reshape(-1)[None, :]
+    )
+    active = jax.nn.gelu(before, approximate=True).astype(jnp.bfloat16)
+    result = (
+        middle + jnp.dot(active, lower, preferred_element_type=jnp.float32) + row_set[7][None, :]
+    )
+
+    final, final_back = jax.vjp(layer_norm, result, tail_rows[0], tail_rows[1])
+    final_low = final.astype(jnp.bfloat16)
+    predict = contract_cols(final_low, head_weight) + head_bias[None, :]
+    difference = predict - targets
+    error_local = jnp.sum(jnp.where(chosen, difference * difference, 0.0))
+    grad_pred = jnp.where(chosen, 2.0 * difference / tile_count, 0.0).astype(jnp.bfloat16)
+    grad_head_bias = jnp.sum(grad_pred, axis=0, dtype=jnp.float32)
+    grad_final = jnp.dot(grad_pred, head_weight, preferred_element_type=jnp.float32)
+    grad_result, grad_gain_last, grad_shift_last = final_back(grad_final)
+
+    grad_out = grad_result.astype(jnp.bfloat16)
+    grad_fc2_bias = jnp.sum(grad_out, axis=0, dtype=jnp.float32)
+    grad_active = contract_cols(grad_out, lower)
+    gelu_value, gelu_back = jax.vjp(partial(jax.nn.gelu, approximate=True), before)
+    grad_before = gelu_back(grad_active)[0].astype(jnp.bfloat16)
+    grad_fc1_bias = jnp.sum(grad_before, axis=0, dtype=jnp.float32)
+    grad_second = contract_cols(grad_before, up_weight)
+    norm_value, norm_back = jax.vjp(layer_norm, middle, row_set[5], row_set[6])
+    grad_middle, grad_gain_two, grad_shift_two = norm_back(grad_second)
+    grad_middle = grad_middle + grad_result
+    grad_branch = grad_middle.astype(jnp.bfloat16)
+    grad_proj_bias = jnp.sum(grad_branch, axis=0, dtype=jnp.float32)
+    grad_mixed = contract_cols(out_weight, grad_branch).astype(jnp.bfloat16)
+    grad_head_out = to_heads(grad_mixed.reshape(HEADS, HEAD_DIM, tok_dev))
+    grad_parts = attend_back(lengths, ids, own_head, grad_head_out, head_out, head_totals)
+    grad_packed = to_heads(grad_parts).reshape(HEADS, 3, HEAD_DIM, tok_dev)
+    grad_packed = grad_packed.swapaxes(0, 1).reshape(3 * D, tok_dev)
+    packed_sums = jnp.sum(grad_packed, axis=1, dtype=jnp.float32)
+    grad_normed = lax.dot_general(
+        grad_packed, qkv_weight, (((0,), (1,)), ((), ())), preferred_element_type=jnp.float32
+    )
+    first_value, first_back = jax.vjp(layer_norm, hidden, row_set[0], row_set[1])
+    grad_hidden, grad_gain_one, grad_shift_one = first_back(grad_normed)
+    grad_hidden = grad_hidden + grad_middle
+    grad_in_low = grad_hidden.astype(jnp.bfloat16)
+    grad_in_bias = jnp.sum(grad_in_low, axis=0, dtype=jnp.float32)
+    grad_inputs = contract_cols(grad_in_low, in_weight)
+    grad_token = jnp.sum(jnp.where(chosen, grad_inputs, 0.0), axis=0)
+
+    index, relative = slot_index(owners, seq_index, core_index, layer_blocks.shape[0])
+    pieces = weight_grads(
+        index,
+        relative,
+        normed.T,
+        grad_packed,
+        mixed_low,
+        grad_branch,
+        second.T,
+        grad_before,
+        active.T,
+        grad_out,
+        inputs.T,
+        grad_in_low,
+        grad_pred.T,
+        final_low,
+    )
+    slot_sum, in_sum, head_sum = reduce_tree(pieces)
+    io_sum = jnp.stack([in_sum, head_sum], axis=1)
+    vec_grads = jnp.concatenate(
+        [
+            jnp.stack(
+                [
+                    grad_gain_one,
+                    grad_shift_one,
+                    packed_sums[:D],
+                    packed_sums[2 * D :],
+                    grad_proj_bias,
+                    grad_gain_two,
+                    grad_shift_two,
+                    grad_fc2_bias,
+                ]
+            ),
+            grad_fc1_bias.reshape(-1, D),
+            jnp.stack([grad_gain_last, grad_shift_last, grad_in_bias]),
+            grad_head_bias.reshape(-1, D),
+            grad_token.reshape(-1, D),
+            jnp.broadcast_to(error_local, (5, D)),
+        ],
+        axis=0,
+    )
+    vec_sum = sum_everywhere(vec_grads)
+    error_sum = vec_sum[vectors.shape[0], 0]
+    vec_sum = vec_sum[: vectors.shape[0]]
+    local_sq = jnp.sum(slot_sum * slot_sum) + jnp.sum(io_sum * io_sum)
+    grad_norm = jnp.sqrt(sum_scalar(local_sq) + jnp.sum(vec_sum * vec_sum))
+    factor = jnp.minimum(1.0, clip_limit / grad_norm)
+    block_grads = slot_sum * factor
+    flipped = block_grads.swapaxes(1, 2)
+    left_new = beta_stat * stat_left + (1.0 - beta_stat) * shampoo_products(block_grads, flipped)
+    right_new = beta_stat * stat_right + (1.0 - beta_stat) * shampoo_products(flipped, block_grads)
+    roots = inverse_roots(jnp.concatenate([left_new, right_new]))
+    slots = left_new.shape[0]
+    direction = shampoo_products(shampoo_products(roots[:slots], block_grads), roots[slots:])
+    blocks_new = layer_blocks - rate_shampoo * direction
+    io_first_new, io_second_new, io_new = adam_update(
+        io_weights, io_first, io_second, io_sum * factor, rate_adam, weight_decay
+    )
+    vec_first_new, vec_second_new, vec_new = adam_update(
+        vectors, vec_first, vec_second, vec_sum * factor, rate_vector, 0.0
+    )
+    return (
+        grad_norm,
+        error_sum,
+        tile_count,
+        block_grads,
+        left_new,
+        right_new,
+        blocks_new,
+        io_first_new,
+        io_second_new,
+        io_new,
+        vec_first_new,
+        vec_second_new,
+        vec_new,
+    )
+
+
 def solution(mesh):
     return jax.shard_map(
-        per_device,
+        fast_device if fits(mesh) else per_device,
         mesh=mesh,
         in_specs=(
             P("opt", "seq", None),

time: 2040 us -> 554 us (0.27)
  waiting for transfers between devices: 822 us -> 148 us
  local copies, waits for them, and re-layouts: 562 us -> 57.9 us
  other arithmetic: 225 us -> 14.3 us
  matrix products: 253 us -> 60.4 us
  Pallas kernels: 0 us -> 163 us
  blocking collectives: 127 us -> 14.6 us
  starting transfers between devices: 9.6 us -> 82.9 us
    reduce_scatter x2 -> x0, waiting for transfers between devices: 343 us -> none  [the longest x1 343 us: per_device(): lax.psum_scatter(slot_grads, ('seq', 'opt'), scatter_dimension=0, tiled=T...]
    all_gather x2 -> x0, waiting for transfers between devices: 189 us -> none  [the longest x1 124 us: per_device(): lax.all_gather(layer_blocks.astype(jnp.bfloat16), ('seq', 'opt'), axis=0,...]
    dot_general x82 -> x30, matrix products: 223 us -> 49.9 us  [the longest x24 32.8 us: shampoo_products(): return jnp.einsum('kij,kjl->kil', left, right, precision=lax.Precision.HIGH)]
    pallas_call x0 -> x16, Pallas kernels: none -> 163 us  [the longest x1 85.1 us: weight_grads(): pl.pallas_call(grads_kernel, out_shape=[jax.ShapeDtypeStruct((4, 2, ROWS,...]
    ppermute x8 -> x61, waiting for transfers between devices: 290 us -> 131 us  [swap(): lax.ppermute(value, axis, [(s, s ^ mask) for s in range(lax.axis_size(axi...]
    another operation x34 -> x5, local copies, waits for them, and re-layouts: 135 us -> 0.17 us  [the longest x4 0.17 us: fast_device(): jnp.stack([grad_gain_one, grad_shift_one, packed_sums[:D], packed_sums[2...]
    psum x2 -> x0, blocking collectives: 127 us -> none  [the longest x1 85.9 us: per_device(): lax.psum(jnp.sum(tile_mask.astype(jnp.float32)), ('seq', 'opt'))]
    scatter x1 -> x2, local copies, waits for them, and re-layouts: 104 us -> 8.08 us  [the longest x1 4.13 us: offsets(): jnp.zeros((768,), jnp.int32).at[owners]]
  transfers between devices with their start and end apart: 12 -> 64, of which waited for: 9 -> 30; matrix products, arithmetic and copies ran while one was open for 20% -> 8% of each run, Pallas kernels for 0% -> 6%
where the time goes in v1:
time: 554 us; the launch traced here: 548 us
  Pallas kernels  163 us (29%)
  waiting for transfers between devices  148 us (27%)
  starting transfers between devices  82.9 us (15%)
  matrix products  60.4 us (11%)
  local copies, waits for them, and re-layouts  57.9 us (10%)
  blocking collectives  14.6 us (3%)
  other arithmetic  14.3 us (3%)
  between operations  6.31 us (1%)
    ppermute x61, waiting for transfers between devices, swap(): lax.ppermute(value, axis, [(s, s ^ mask) for s in range(lax.axis_size(axi...  131 us
    pallas_call x1, Pallas kernels, weight_grads(): pl.pallas_call(grads_kernel, out_shape=[jax.ShapeDtypeStruct((4, 2, ROWS,...  85.1 us
    ppermute x61, starting transfers between devices, swap(): lax.ppermute(value, axis, [(s, s ^ mask) for s in range(lax.axis_size(axi...  68.4 us
    unnamed x156, local copies, waits for them, and re-layouts  34.8 us
    dot_general x24, matrix products, shampoo_products(): return jnp.einsum('kij,kjl->kil', left, right, precision=lax.Precision.HIGH)  32.8 us
    pallas_call x1, Pallas kernels, join_weights(): pl.pallas_call(partial(assemble_kernel, n), out_shape=[jax.ShapeDtypeStru...  29.4 us
    pallas_call x12, Pallas kernels, code_call(): pl.pallas_call(kernel, out_shape=[jax.ShapeDtypeStruct(s, t) for s, t in...  22.5 us
    all_to_all x3, waiting for transfers between devices, to_heads(): return lax.all_to_all(parts, 'seq', 0, 0, tiled=True)  17.7 us
  transfers between devices with their start and end apart: 64, of which 30 were waited for; matrix products, arithmetic and copies ran while one was open for 8% of the time, Pallas kernels for 6%

profile of v1, /device:TPU:0, one launch (start us, length us, event | category | flops | bytes accessed | tf_op | source)
XLA Modules:
  0.0 547.8 jit_solution(13592546202124803629)
XLA Ops:
  6.4 4.0 collective-permute-start.9
  15.9 4.5 collective-permute-done
  25.1 11.5 %collective-permute-done.9 = bf16[768,384]{1,0:T(8,128)(2,1)S(1)} collective-permute-done((bf16[768,384]{1,0:T(8,128)(2,1)S(1)}, bf16[768,384]{1,0:T(8,128)(2,1)S(1)}, u32[]{:S(2)}, u32[]{:S(2)}) %collective-permute-start.9) | collective-permute-done | bytes 589856 | tf_op jit(solution)/shard_map/ppermute | solution.py:565
  36.6 1.6 collective-permute-start.10
  42.2 4.4 collective-permute-done.10
  52.4 2.1 collective-permute-done.6
  54.6 2.2 collective-permute-start.13
  64.8 9.8 %collective-permute-done.15 = bf16[384,384]{1,0:T(8,128)(2,1)S(1)} collective-permute-done((bf16[384,384]{1,0:T(8,128)(2,1)S(1)}, bf16[384,384]{1,0:T(8,128)(2,1)S(1)}, u32[]{:S(2)}, u32[]{:S(2)}) %collective-permute-start.15) | collective-permute-done | bytes 294944 | tf_op jit(solution)/shard_map/ppermute | solution.py:565
  74.5 2.0 collective-permute-start.8
  76.6 8.3 %collective-permute-done.16 = bf16[384,384]{1,0:T(8,128)(2,1)S(1)} collective-permute-done((bf16[384,384]{1,0:T(8,128)(2,1)S(1)}, bf16[384,384]{1,0:T(8,128)(2,1)S(1)}, u32[]{:S(2)}, u32[]{:S(2)}) %collective-permute-start.16) | collective-permute-done | bytes 294944 | tf_op jit(solution)/shard_map/ppermute | solution.py:565
  85.0 1.6 collective-permute-start.17
  93.8 7.1 %collective-permute-done.17 = bf16[768,384]{1,0:T(8,128)(2,1)S(1)} collective-permute-done((bf16[768,384]{1,0:T(8,128)(2,1)S(1)}, bf16[768,384]{1,0:T(8,128)(2,1)S(1)}, u32[]{:S(2)}, u32[]{:S(2)}) %collective-permute-start.17) | collective-permute-done | bytes 589856 | tf_op jit(solution)/shard_map/ppermute | solution.py:565
  105.6 4.1 scatter_custom_fusion.1.index_ref
  111.5 29.4 %join_weights.1 = (bf16[768,6144]{1,0:T(8,128)(2,1)}, bf16[3072,768]{1,0:T(8,128)(2,1)}, bf16[1536,768]{1,0:T(8,128)(2,1)}, bf16[1536,768]{1,0:T(8,128)(2,1)}) custom-call(s32[768]{0:T(1024)} %scatter_custom_fusion.1.index_ref, s32[2,32]{1,0:T(2,128)} %pad_add_fusion.io_ref, bf16[3072,384]{1,0:T(8,128)(2,1)} %constant_dynamic-update-slice_fusion.refs_0_, ...), custom_call_target="tpu_custom_call" | custom-call | tf_op jit(solution)/shard_map/join_weights/pallas_call | solution.py:646
  140.9 2.5 fusion.170
  144.3 3.4 fusion.7
  148.5 6.0 %all-to-all-start = ((bf16[16,144,128]{2,1,0:T(8,128)(2,1)}), bf16[16,144,128]{2,1,0:T(8,128)(2,1)S(1)}, u32[]{:S(2)}, u32[]{:S(2)}) async-start(bf16[16,144,128]{2,1,0:T(8,128)(2,1)} %bitcast.16), calls=%async_computation | async-start | bytes 1179648 | tf_op jit(solution)/shard_map/all_to_all | solution.py:1040
  156.2 15.0 %all-to-all-done.qkv_ref = bf16[16,144,128]{2,1,0:T(8,128)(2,1)S(1)} async-done(((bf16[16,144,128]{2,1,0:T(8,128)(2,1)}), bf16[16,144,128]{2,1,0:T(8,128)(2,1)S(1)}, u32[]{:S(2)}, u32[]{:S(2)}) %all-to-all-start) | async-done | bytes 589856 | tf_op jit(solution)/shard_map/all_to_all | solution.py:1040
  171.2 11.5 %attend_forward.1 = (f32[48,2048]{1,0:T(8,128)S(1)}, bf16[16,48,128]{2,1,0:T(8,128)(2,1)}, f32[8,2048]{1,0:T(8,128)S(1)}) custom-call(s32[2,4]{1,0:T(2,128)S(1)} %copy-done.20, s32[2]{0:T(128)S(1)} %pad_add_fusion.1.ids_ref, bf16[16,144,128]{2,1,0:T(8,128)(2,1)S(1)} %all-to-all-done.qkv_ref), custom_call_target="tpu_custom_call" | custom-call | tf_op jit(solution)/shard_map/attend_forward/pallas_call | solution.py:833
  182.7 4.9 all-to-all-start.1
  188.3 2.1 collective-permute-start.24
  192.6 2.5 collective-permute-start.25
  196.7 1.7 collective-permute-start.26
  198.4 1.9 collective-permute-done.26
  200.3 2.6 collective-permute-start.27
  203.0 1.8 collective-permute-done.27
  205.3 1.8 fusion.171
  207.4 5.6 %fusion.46 = (bf16[3072,128]{1,0:T(8,128)(2,1)}, f32[128,3072]{0,1:T(8,128)S(1)}) fusion(f32[3072]{0:T(1024)S(1)} %add.522, bf16[768,6144]{1,0:T(8,128)(2,1)} %get-tuple-element.64, f32[128,768]{1,0:T(8,128)S(1)} %get-tuple-element.241, f32[768]{0:T(1024)S(1)} %get-tuple-element.177, f32[768]{0:T(1024)S(1)} %get-tuple-element.178, f32[128]{0:T(128)S(1)} %fusion.133, ...), kind=kOutput, calls=%fused_computation.58 | convolution fusion | flops 608403456 | bytes 7490560 | tf_op jit(solution)/shard_map/dot_general | solution.py:1120
  214.7 2.2 convert_reduce_fusion.2
  218.0 1.9 convert_reduce_fusion
  219.9 2.4 multiply_reduce_fusion.3
  223.2 14.6 %all_to_all.20.do_ref = bf16[16,48,128]{2,1,0:T(8,128)(2,1)S(1)} all-to-all(bf16[16,48,128]{2,1,0:T(8,128)(2,1)S(1)} %bitcast.110), channel_id=1, replica_groups=mesh['seq'=16,'opt'=2] {'seq'}, dimensions={0} | all-to-all | bytes 393216 | tf_op jit(solution)/shard_map/all_to_all | solution.py:1040
  237.9 14.5 %attend_backward.1 = bf16[16,144,128]{2,1,0:T(8,128)(2,1)} custom-call(s32[2,4]{1,0:T(2,128)S(1)} %copy-done.20, s32[2]{0:T(128)S(1)} %pad_add_fusion.1.ids_ref, bf16[16,144,128]{2,1,0:T(8,128)(2,1)S(1)} %all-to-all-done.qkv_ref, bf16[16,48,128]{2,1,0:T(8,128)(2,1)S(1)} %all_to_all.20.do_ref, f32[48,2048]{1,0:T(8,128)S(1)} %get-tuple-element.68.o_ref, ...), custom_call_target="tpu_custom_call" | custom-call | tf_op jit(solution)/shard_map/attend_backward/pallas_call | solution.py:840
  252.4 3.6 all-to-all-start.3
  256.0 3.9 scatter_custom_fusion.index_ref
  261.5 2.3 copy.109.refs_5_
  264.6 2.7 all-to-all-done.3
  267.4 3.8 multiply_reduce_fusion.4
  273.2 85.1 %weight_grads.1 = (s16[4,2,400,384]{3,2,1,0:T(8,128)(2,1)}, s16[4,2,400,384]{3,2,1,0:T(8,128)(2,1)}, s16[4,2,400,384]{3,2,1,0:T(8,128)(2,1)}, s16[4,2,400,384]{3...) custom-call(s32[768]{0:T(1024)} %scatter_custom_fusion.index_ref, ...), custom_call_target="tpu_custom_call" | custom-call | tf_op jit(solution)/shard_map/weight_grads/pallas_call | solution.py:930
  359.4 3.9 collective-permute-done.44.theirs
  363.3 1.7 copy-done.3
  365.0 2.2 split_halves.7
  368.9 2.2 split_halves.5
  371.1 1.9 collective-permute-start.34
  373.7 2.2 split_halves.6
  375.9 8.1 %collective-permute-done.45.got_a = s16[2,400,384]{2,1,0:T(8,128)(2,1)S(1)} collective-permute-done((s16[2,400,384]{2,1,0:T(8,128)(2,1)S(1)}, s16[2,400,384]{2,1,0:T(8,128)(2,1)S(1)}, u32[]{:S(2)}, u32[]{:S(2)}) %collective-permute-start.45) | collective-permute-done | bytes 614432 | tf_op jit(solution)/shard_map/ppermute | solution.py:565
  386.7 10.4 %collective-permute-done.34.got_a = s16[2,400,384]{2,1,0:T(8,128)(2,1)S(1)} collective-permute-done((s16[2,400,384]{2,1,0:T(8,128)(2,1)S(1)}, s16[2,400,384]{2,1,0:T(8,128)(2,1)S(1)}, u32[]{:S(2)}, u32[]{:S(2)}) %collective-permute-start.34) | collective-permute-done | bytes 614432 | tf_op jit(solution)/shard_map/ppermute | solution.py:565
  400.4 16.5 %collective-permute-done.47.refs_1_ = s16[400,384]{1,0:T(8,128)(2,1)S(1)} collective-permute-done((s16[400,384]{1,0:T(8,128)(2,1)S(1)}, s16[400,384]{1,0:T(8,128)(2,1)S(1)}, u32[]{:S(2)}, u32[]{:S(2)}) %collective-permute-start.47) | collective-permute-done | bytes 307232 | tf_op jit(solution)/shard_map/ppermute | solution.py:565
  417.5 1.7 collective-permute-start.37
  420.5 3.6 split_halves.4
  426.6 1.9 add_plane.6
  436.7 8.9 %collective-permute-done.42.refs_1_ = s16[400,384]{1,0:T(8,128)(2,1)S(1)} collective-permute-done((s16[400,384]{1,0:T(8,128)(2,1)}, s16[400,384]{1,0:T(8,128)(2,1)S(1)}, u32[]{:S(2)}, u32[]{:S(2)}) %collective-permute-start.42) | collective-permute-done | bytes 307232 | tf_op jit(solution)/shard_map/ppermute | solution.py:565
  450.2 2.9 add_line.5
  454.1 1.8 fusion.50
  455.9 3.2 add_plane.4
  468.3 11.7 %collective-permute-done.50.refs_5_ = s16[2,400,384]{2,1,0:T(8,128)(2,1)S(1)} collective-permute-done((s16[2,400,384]{2,1,0:T(8,128)(2,1)}, s16[2,400,384]{2,1,0:T(8,128)(2,1)S(1)}, u32[]{:S(2)}, u32[]{:S(2)}) %collective-permute-start.50) | collective-permute-done | bytes 614432 | tf_op jit(solution)/shard_map/ppermute | solution.py:565
  488.8 2.6 collective-permute-done.58
  492.9 2.9 collective-permute-done.59
  496.3 2.0 collective-permute-start.54
  498.4 3.0 collective-permute-done.60
  503.6 2.4 collective-permute-done.55
  514.4 1.9 fusion.15
  535.2 1.7 fusion.17
  543.7 1.8 fusion.47
  (411 shorter events, 145.2 us)
Async XLA Ops:
  6.4 30.1 %collective-permute-start.9 = (bf16[768,384]{1,0:T(8,128)(2,1)S(1)}, bf16[768,384]{1,0:T(8,128)(2,1)S(1)}, u32[]{:S(2)}, u32[]{:S(2)}) collective-permute-start(bf16[768,384]{1,0:T(8,128)(2,1)S(1)} %get-tuple-element.224), channel_id=1, source_target_pairs={{0,16},{2,18},{4,20},{6,22},{8,24},{10,26},{12,28},{14,30},{16,0},... | collective-permute-start | bytes 1769480 | tf_op jit(solution)/shard_map/ppermute | solution.py:565
  10.5 29.3 %collective-permute-start.4 = (bf16[768,384]{1,0:T(8,128)(2,1)S(1)}, bf16[768,384]{1,0:T(8,128)(2,1)S(1)}, u32[]{:S(2)}, u32[]{:S(2)}) collective-permute-start(bf16[768,384]{1,0:T(8,128)(2,1)S(1)} %get-tuple-element.224), channel_id=1, source_target_pairs={{0,8},{2,10},{4,12},{6,14},{8,0},{10,2},{12,4},{14,6},{16,24},{18,... | collective-permute-start | bytes 1769480 | tf_op jit(solution)/shard_map/ppermute | solution.py:565
  12.1 8.3 %collective-permute-start = (bf16[384,384]{1,0:T(8,128)(2,1)S(1)}, bf16[384,384]{1,0:T(8,128)(2,1)S(1)}, u32[]{:S(2)}, u32[]{:S(2)}) collective-permute-start(bf16[384,384]{1,0:T(8,128)(2,1)S(1)} %pad_maximum_fusion.8), channel_id=1, source_target_pairs={{0,2},{2,0},{4,6},{6,4},{8,10},{10,8},{12,14},{14,12},{16,18},{18,... | collective-permute-start | bytes 884744 | tf_op jit(solution)/shard_map/ppermute | solution.py:565
  13.7 8.3 %collective-permute-start.1 = (bf16[384,384]{1,0:T(8,128)(2,1)S(1)}, bf16[384,384]{1,0:T(8,128)(2,1)S(1)}, u32[]{:S(2)}, u32[]{:S(2)}) collective-permute-start(bf16[384,384]{1,0:T(8,128)(2,1)S(1)} %pad_maximum_fusion.9), channel_id=1, source_target_pairs={{0,4},{2,6},{4,0},{6,2},{8,12},{10,14},{12,8},{14,10},{16,20},{18,... | collective-permute-start | bytes 884744 | tf_op jit(solution)/shard_map/ppermute | solution.py:565
  20.4 36.4 %collective-permute-start.2 = (bf16[768,384]{1,0:T(8,128)(2,1)S(1)}, bf16[768,384]{1,0:T(8,128)(2,1)S(1)}, u32[]{:S(2)}, u32[]{:S(2)}) collective-permute-start(bf16[768,384]{1,0:T(8,128)(2,1)S(1)} %pad_maximum_fusion), channel_id=1, source_target_pairs={{0,4},{2,6},{4,0},{6,2},{8,12},{10,14},{12,8},{14,10},{16,20},{18,... | collective-permute-start | bytes 1769480 | tf_op jit(solution)/shard_map/ppermute | solution.py:565
  22.0 37.2 %collective-permute-start.3 = (bf16[768,384]{1,0:T(8,128)(2,1)S(1)}, bf16[768,384]{1,0:T(8,128)(2,1)S(1)}, u32[]{:S(2)}, u32[]{:S(2)}) collective-permute-start(bf16[768,384]{1,0:T(8,128)(2,1)S(1)} %pad_maximum_fusion.1), channel_id=1, source_target_pairs={{0,2},{2,0},{4,6},{6,4},{8,10},{10,8},{12,14},{14,12},{16,18},{18,... | collective-permute-start | bytes 1769480 | tf_op jit(solution)/shard_map/ppermute | solution.py:565
  36.6 10.0 %collective-permute-start.10 = (bf16[384,384]{1,0:T(8,128)(2,1)S(1)}, bf16[384,384]{1,0:T(8,128)(2,1)S(1)}, u32[]{:S(2)}, u32[]{:S(2)}) collective-permute-start(bf16[384,384]{1,0:T(8,128)(2,1)S(1)} %get-tuple-element.211), channel_id=1, source_target_pairs={{0,2},{2,0},{4,6},{6,4},{8,10},{10,8},{12,14},{14,12},{16,18},{18,... | collective-permute-start | bytes 884744 | tf_op jit(solution)/shard_map/ppermute | solution.py:565
  38.2 10.0 %collective-permute-start.11 = (bf16[384,384]{1,0:T(8,128)(2,1)S(1)}, bf16[384,384]{1,0:T(8,128)(2,1)S(1)}, u32[]{:S(2)}, u32[]{:S(2)}) collective-permute-start(bf16[384,384]{1,0:T(8,128)(2,1)S(1)} %get-tuple-element.210), channel_id=1, source_target_pairs={{0,4},{2,6},{4,0},{6,2},{8,12},{10,14},{12,8},{14,10},{16,20},{18,... | collective-permute-start | bytes 884744 | tf_op jit(solution)/shard_map/ppermute | solution.py:565
  39.8 11.3 %collective-permute-start.5 = (bf16[384,384]{1,0:T(8,128)(2,1)S(1)}, bf16[384,384]{1,0:T(8,128)(2,1)S(1)}, u32[]{:S(2)}, u32[]{:S(2)}) collective-permute-start(bf16[384,384]{1,0:T(8,128)(2,1)S(1)} %get-tuple-element.213), channel_id=1, source_target_pairs={{0,2},{2,0},{4,6},{6,4},{8,10},{10,8},{12,14},{14,12},{16,18},{18,... | collective-permute-start | bytes 884744 | tf_op jit(solution)/shard_map/ppermute | solution.py:565
  46.6 8.0 %collective-permute-start.6 = (bf16[384,384]{1,0:T(8,128)(2,1)S(1)}, bf16[384,384]{1,0:T(8,128)(2,1)S(1)}, u32[]{:S(2)}, u32[]{:S(2)}) collective-permute-start(bf16[384,384]{1,0:T(8,128)(2,1)S(1)} %get-tuple-element.212), channel_id=1, source_target_pairs={{0,4},{2,6},{4,0},{6,2},{8,12},{10,14},{12,8},{14,10},{16,20},{18,... | collective-permute-start | bytes 884744 | tf_op jit(solution)/shard_map/ppermute | solution.py:565
  48.2 12.0 %collective-permute-start.14 = (bf16[768,384]{1,0:T(8,128)(2,1)S(1)}, bf16[768,384]{1,0:T(8,128)(2,1)S(1)}, u32[]{:S(2)}, u32[]{:S(2)}) collective-permute-start(bf16[768,384]{1,0:T(8,128)(2,1)S(1)} %collective-permute-done.9), channel_id=1, source_target_pairs={{0,8},{2,10},{4,12},{6,14},{8,0},{10,2},{12,4},{14,6},{16,24},{18,... | collective-permute-start | bytes 1769480 | tf_op jit(solution)/shard_map/ppermute | solution.py:565
  51.1 33.9 %collective-permute-start.12 = (bf16[768,384]{1,0:T(8,128)(2,1)S(1)}, bf16[768,384]{1,0:T(8,128)(2,1)S(1)}, u32[]{:S(2)}, u32[]{:S(2)}) collective-permute-start(bf16[768,384]{1,0:T(8,128)(2,1)S(1)} %pad_maximum_fusion.4), channel_id=1, source_target_pairs={{0,4},{2,6},{4,0},{6,2},{8,12},{10,14},{12,8},{14,10},{16,20},{18,... | collective-permute-start | bytes 1769480 | tf_op jit(solution)/shard_map/ppermute | solution.py:565
  54.6 33.0 %collective-permute-start.13 = (bf16[768,384]{1,0:T(8,128)(2,1)S(1)}, bf16[768,384]{1,0:T(8,128)(2,1)S(1)}, u32[]{:S(2)}, u32[]{:S(2)}) collective-permute-start(bf16[768,384]{1,0:T(8,128)(2,1)S(1)} %pad_maximum_fusion.5), channel_id=1, source_target_pairs={{0,2},{2,0},{4,6},{6,4},{8,10},{10,8},{12,14},{14,12},{16,18},{18,... | collective-permute-start | bytes 1769480 | tf_op jit(solution)/shard_map/ppermute | solution.py:565
  56.8 33.1 %collective-permute-start.7 = (bf16[768,384]{1,0:T(8,128)(2,1)S(1)}, bf16[768,384]{1,0:T(8,128)(2,1)S(1)}, u32[]{:S(2)}, u32[]{:S(2)}) collective-permute-start(bf16[768,384]{1,0:T(8,128)(2,1)S(1)} %pad_maximum_fusion.2), channel_id=1, source_target_pairs={{0,4},{2,6},{4,0},{6,2},{8,12},{10,14},{12,8},{14,10},{16,20},{18,... | collective-permute-start | bytes 1769480 | tf_op jit(solution)/shard_map/ppermute | solution.py:565
  60.3 14.2 %collective-permute-start.15 = (bf16[384,384]{1,0:T(8,128)(2,1)S(1)}, bf16[384,384]{1,0:T(8,128)(2,1)S(1)}, u32[]{:S(2)}, u32[]{:S(2)}) collective-permute-start(bf16[384,384]{1,0:T(8,128)(2,1)S(1)} %get-tuple-element.209), channel_id=1, source_target_pairs={{0,2},{2,0},{4,6},{6,4},{8,10},{10,8},{12,14},{14,12},{16,18},{18,... | collective-permute-start | bytes 884744 | tf_op jit(solution)/shard_map/ppermute | solution.py:565
  62.6 22.3 %collective-permute-start.16 = (bf16[384,384]{1,0:T(8,128)(2,1)S(1)}, bf16[384,384]{1,0:T(8,128)(2,1)S(1)}, u32[]{:S(2)}, u32[]{:S(2)}) collective-permute-start(bf16[384,384]{1,0:T(8,128)(2,1)S(1)} %get-tuple-element.208), channel_id=1, source_target_pairs={{0,4},{2,6},{4,0},{6,2},{8,12},{10,14},{12,8},{14,10},{16,20},{18,... | collective-permute-start | bytes 884744 | tf_op jit(solution)/shard_map/ppermute | solution.py:565
  74.5 16.3 %collective-permute-start.8 = (bf16[768,384]{1,0:T(8,128)(2,1)S(1)}, bf16[768,384]{1,0:T(8,128)(2,1)S(1)}, u32[]{:S(2)}, u32[]{:S(2)}) collective-permute-start(bf16[768,384]{1,0:T(8,128)(2,1)S(1)} %pad_maximum_fusion.3), channel_id=1, source_target_pairs={{0,2},{2,0},{4,6},{6,4},{8,10},{10,8},{12,14},{14,12},{16,18},{18,... | collective-permute-start | bytes 1769480 | tf_op jit(solution)/shard_map/ppermute | solution.py:565
  84.9 26.5 %collective-permute-start.19 = (bf16[3072,384]{1,0:T(8,128)(2,1)}, bf16[3072,384]{1,0:T(8,128)(2,1)}, u32[]{:S(2)}, u32[]{:S(2)}) collective-permute-start(bf16[3072,384]{1,0:T(8,128)(2,1)} %constant_dynamic-update-slice_fusion.refs_0_), channel_id=1, source_target_pairs={{0,1},{1,0},{2,3},{3,2},{4,5},{5,4},{6,7},{7,6},{8,9},{9,8},{10,11... | collective-permute-start | bytes 7077896 | tf_op jit(solution)/shard_map/ppermute | solution.py:565
  85.0 15.8 %collective-permute-start.17 = (bf16[768,384]{1,0:T(8,128)(2,1)S(1)}, bf16[768,384]{1,0:T(8,128)(2,1)S(1)}, u32[]{:S(2)}, u32[]{:S(2)}) collective-permute-start(bf16[768,384]{1,0:T(8,128)(2,1)S(1)} %pad_maximum_fusion.6), channel_id=1, source_target_pairs={{0,4},{2,6},{4,0},{6,2},{8,12},{10,14},{12,8},{14,10},{16,20},{18,... | collective-permute-start | bytes 1769480 | tf_op jit(solution)/shard_map/ppermute | solution.py:565
  87.6 15.5 %collective-permute-start.18 = (bf16[768,384]{1,0:T(8,128)(2,1)S(1)}, bf16[768,384]{1,0:T(8,128)(2,1)S(1)}, u32[]{:S(2)}, u32[]{:S(2)}) collective-permute-start(bf16[768,384]{1,0:T(8,128)(2,1)S(1)} %pad_maximum_fusion.7), channel_id=1, source_target_pairs={{0,2},{2,0},{4,6},{6,4},{8,10},{10,8},{12,14},{14,12},{16,18},{18,... | collective-permute-start | bytes 1769480 | tf_op jit(solution)/shard_map/ppermute | solution.py:565
  89.9 21.5 %collective-permute-start.21 = (bf16[3072,384]{1,0:T(8,128)(2,1)}, bf16[3072,384]{1,0:T(8,128)(2,1)}, u32[]{:S(2)}, u32[]{:S(2)}) collective-permute-start(bf16[3072,384]{1,0:T(8,128)(2,1)} %constant_dynamic-update-slice_fusion.21.refs_2_), channel_id=1, source_target_pairs={{0,1},{1,0},{2,3},{3,2},{4,5},{5,4},{6,7},{7,6},{8,9},{9,8},{10,11... | collective-permute-start | bytes 7077896 | tf_op jit(solution)/shard_map/ppermute | solution.py:565
  91.7 19.7 %collective-permute-start.20 = (bf16[3072,384]{1,0:T(8,128)(2,1)}, bf16[3072,384]{1,0:T(8,128)(2,1)}, u32[]{:S(2)}, u32[]{:S(2)}) collective-permute-start(bf16[3072,384]{1,0:T(8,128)(2,1)} %constant_dynamic-update-slice_fusion.16.refs_1_), channel_id=1, source_target_pairs={{0,1},{1,0},{2,3},{3,2},{4,5},{5,4},{6,7},{7,6},{8,9},{9,8},{10,11... | collective-permute-start | bytes 7077896 | tf_op jit(solution)/shard_map/ppermute | solution.py:565
  103.9 7.6 %collective-permute-start.22 = (bf16[3072,384]{1,0:T(8,128)(2,1)}, bf16[3072,384]{1,0:T(8,128)(2,1)}, u32[]{:S(2)}, u32[]{:S(2)}) collective-permute-start(bf16[3072,384]{1,0:T(8,128)(2,1)} %constant_dynamic-update-slice_fusion.26.refs_3_), channel_id=1, source_target_pairs={{0,1},{1,0},{2,3},{3,2},{4,5},{5,4},{6,7},{7,6},{8,9},{9,8},{10,11... | collective-permute-start | bytes 7077896 | tf_op jit(solution)/shard_map/ppermute | solution.py:565
  148.5 22.6 %all-to-all-start = ((bf16[16,144,128]{2,1,0:T(8,128)(2,1)}), bf16[16,144,128]{2,1,0:T(8,128)(2,1)S(1)}, u32[]{:S(2)}, u32[]{:S(2)}) async-start(bf16[16,144,128]{2,1,0:T(8,128)(2,1)} %bitcast.16), calls=%async_computation | async-start | bytes 1179648 | tf_op jit(solution)/shard_map/all_to_all | solution.py:1040
  155.8 31.8 %collective-permute-start.23 = (f32[8,128]{1,0:T(8,128)S(1)}, f32[8,128]{1,0:T(8,128)S(1)}, u32[]{:S(2)}, u32[]{:S(2)}) collective-permute-start(f32[8,128]{1,0:T(8,128)S(1)} %broadcast_in_dim.152), channel_id=1, source_target_pairs={{0,1},{1,0},{2,3},{3,2},{4,5},{5,4},{6,7},{7,6},{8,9},{9,8},{10,11... | collective-permute-start | bytes 12296 | tf_op jit(solution)/shard_map/ppermute | solution.py:565
  182.7 22.6 %all-to-all-start.1 = ((bf16[16,48,128]{2,1,0:T(8,128)(2,1)}), bf16[16,48,128]{2,1,0:T(8,128)(2,1)S(1)}, u32[]{:S(2)}, u32[]{:S(2)}) async-start(bf16[16,48,128]{2,1,0:T(8,128)(2,1)} %get-tuple-element.65), calls=%async_computation.1 | async-start | bytes 393216 | tf_op jit(solution)/shard_map/all_to_all | solution.py:1040
  188.3 3.7 collective-permute-start.24
  192.6 4.1 collective-permute-start.25
  196.7 3.6 collective-permute-start.26
  200.3 4.5 collective-permute-start.27
  252.4 15.0 %all-to-all-start.3 = ((bf16[16,144,128]{2,1,0:T(8,128)(2,1)}), bf16[16,144,128]{2,1,0:T(8,128)(2,1)S(1)}, u32[]{:S(2)}, u32[]{:S(2)}) async-start(bf16[16,144,128]{2,1,0:T(8,128)(2,1)} %attend_backward.1), calls=%async_computation.3 | async-start | bytes 1179648 | tf_op jit(solution)/shard_map/all_to_all | solution.py:1040
  358.3 5.0 collective-permute-start.44
  358.4 10.4 %collective-permute-start.33 = (s16[4,2,400,384]{3,2,1,0:T(8,128)(2,1)}, s16[4,2,400,384]{3,2,1,0:T(8,128)(2,1)S(1)}, u32[]{:S(2)}, u32[]{:S(2)}) collective-permute-start(s16[4,2,400,384]{3,2,1,0:T(8,128)(2,1)} %get-tuple-element.81), channel_id=1, source_target_pairs={{0,1},{1,0},{2,3},{3,2},{4,5},{5,4},{6,7},{7,6},{8,9},{9,8},{10,11... | collective-permute-start | bytes 7372808 | tf_op jit(solution)/shard_map/ppermute | solution.py:565
  358.9 14.1 %collective-permute-start.39 = (s16[4,2,400,384]{3,2,1,0:T(8,128)(2,1)}, s16[4,2,400,384]{3,2,1,0:T(8,128)(2,1)S(1)}, u32[]{:S(2)}, u32[]{:S(2)}) collective-permute-start(s16[4,2,400,384]{3,2,1,0:T(8,128)(2,1)} %get-tuple-element.91), channel_id=1, source_target_pairs={{0,1},{1,0},{2,3},{3,2},{4,5},{5,4},{6,7},{7,6},{8,9},{9,8},{10,11... | collective-permute-start | bytes 7372808 | tf_op jit(solution)/shard_map/ppermute | solution.py:565
  359.0 60.8 %collective-permute-start.28 = (s16[4,2,400,384]{3,2,1,0:T(8,128)(2,1)}, s16[4,2,400,384]{3,2,1,0:T(8,128)(2,1)S(1)}, u32[]{:S(2)}, u32[]{:S(2)}) collective-permute-start(s16[4,2,400,384]{3,2,1,0:T(8,128)(2,1)} %get-tuple-element.71), channel_id=1, source_target_pairs={{0,1},{1,0},{2,3},{3,2},{4,5},{5,4},{6,7},{7,6},{8,9},{9,8},{10,11... | collective-permute-start | bytes 7372808 | tf_op jit(solution)/shard_map/ppermute | solution.py:565
  367.2 16.8 %collective-permute-start.45 = (s16[2,400,384]{2,1,0:T(8,128)(2,1)S(1)}, s16[2,400,384]{2,1,0:T(8,128)(2,1)S(1)}, u32[]{:S(2)}, u32[]{:S(2)}) collective-permute-start(s16[2,400,384]{2,1,0:T(8,128)(2,1)S(1)} %get-tuple-element.103), channel_id=1, source_target_pairs={{0,4},{2,6},{4,0},{6,2},{8,12},{10,14},{12,8},{14,10},{16,20},{18,... | collective-permute-start | bytes 1843208 | tf_op jit(solution)/shard_map/ppermute | solution.py:565
  368.3 16.7 %collective-permute-start.46 = (s16[2,400,384]{2,1,0:T(8,128)(2,1)S(1)}, s16[2,400,384]{2,1,0:T(8,128)(2,1)S(1)}, u32[]{:S(2)}, u32[]{:S(2)}) collective-permute-start(s16[2,400,384]{2,1,0:T(8,128)(2,1)S(1)} %get-tuple-element.105), channel_id=1, source_target_pairs={{0,2},{2,0},{4,6},{6,4},{8,10},{10,8},{12,14},{14,12},{16,18},{18,... | collective-permute-start | bytes 1843208 | tf_op jit(solution)/shard_map/ppermute | solution.py:565
  371.1 26.0 %collective-permute-start.34 = (s16[2,400,384]{2,1,0:T(8,128)(2,1)S(1)}, s16[2,400,384]{2,1,0:T(8,128)(2,1)S(1)}, u32[]{:S(2)}, u32[]{:S(2)}) collective-permute-start(s16[2,400,384]{2,1,0:T(8,128)(2,1)S(1)} %get-tuple-element.83), channel_id=1, source_target_pairs={{0,4},{2,6},{4,0},{6,2},{8,12},{10,14},{12,8},{14,10},{16,20},{18,... | collective-permute-start | bytes 1843208 | tf_op jit(solution)/shard_map/ppermute | solution.py:565
  373.0 25.5 %collective-permute-start.35 = (s16[2,400,384]{2,1,0:T(8,128)(2,1)S(1)}, s16[2,400,384]{2,1,0:T(8,128)(2,1)S(1)}, u32[]{:S(2)}, u32[]{:S(2)}) collective-permute-start(s16[2,400,384]{2,1,0:T(8,128)(2,1)S(1)} %get-tuple-element.85), channel_id=1, source_target_pairs={{0,2},{2,0},{4,6},{6,4},{8,10},{10,8},{12,14},{14,12},{16,18},{18,... | collective-permute-start | bytes 1843208 | tf_op jit(solution)/shard_map/ppermute | solution.py:565
  384.0 40.1 %collective-permute-start.40 = (s16[2,400,384]{2,1,0:T(8,128)(2,1)S(1)}, s16[2,400,384]{2,1,0:T(8,128)(2,1)S(1)}, u32[]{:S(2)}, u32[]{:S(2)}) collective-permute-start(s16[2,400,384]{2,1,0:T(8,128)(2,1)S(1)} %get-tuple-element.93), channel_id=1, source_target_pairs={{0,4},{2,6},{4,0},{6,2},{8,12},{10,14},{12,8},{14,10},{16,20},{18,... | collective-permute-start | bytes 1843208 | tf_op jit(solution)/shard_map/ppermute | solution.py:565
  385.0 40.1 %collective-permute-start.41 = (s16[2,400,384]{2,1,0:T(8,128)(2,1)S(1)}, s16[2,400,384]{2,1,0:T(8,128)(2,1)S(1)}, u32[]{:S(2)}, u32[]{:S(2)}) collective-permute-start(s16[2,400,384]{2,1,0:T(8,128)(2,1)S(1)} %get-tuple-element.95), channel_id=1, source_target_pairs={{0,2},{2,0},{4,6},{6,4},{8,10},{10,8},{12,14},{14,12},{16,18},{18,... | collective-permute-start | bytes 1843208 | tf_op jit(solution)/shard_map/ppermute | solution.py:565
  397.2 19.7 %collective-permute-start.47 = (s16[400,384]{1,0:T(8,128)(2,1)S(1)}, s16[400,384]{1,0:T(8,128)(2,1)S(1)}, u32[]{:S(2)}, u32[]{:S(2)}) collective-permute-start(s16[400,384]{1,0:T(8,128)(2,1)S(1)} %get-tuple-element.107), channel_id=1, source_target_pairs={{0,2},{2,0},{4,6},{6,4},{8,10},{10,8},{12,14},{14,12},{16,18},{18,... | collective-permute-start | bytes 921608 | tf_op jit(solution)/shard_map/ppermute | solution.py:565
  398.5 19.0 %collective-permute-start.48 = (s16[400,384]{1,0:T(8,128)(2,1)S(1)}, s16[400,384]{1,0:T(8,128)(2,1)S(1)}, u32[]{:S(2)}, u32[]{:S(2)}) collective-permute-start(s16[400,384]{1,0:T(8,128)(2,1)S(1)} %get-tuple-element.109), channel_id=1, source_target_pairs={{0,4},{2,6},{4,0},{6,2},{8,12},{10,14},{12,8},{14,10},{16,20},{18,... | collective-permute-start | bytes 921608 | tf_op jit(solution)/shard_map/ppermute | solution.py:565
  416.8 13.2 %collective-permute-start.36 = (s16[400,384]{1,0:T(8,128)(2,1)S(1)}, s16[400,384]{1,0:T(8,128)(2,1)S(1)}, u32[]{:S(2)}, u32[]{:S(2)}) collective-permute-start(s16[400,384]{1,0:T(8,128)(2,1)S(1)} %get-tuple-element.87), channel_id=1, source_target_pairs={{0,2},{2,0},{4,6},{6,4},{8,10},{10,8},{12,14},{14,12},{16,18},{18,... | collective-permute-start | bytes 921608 | tf_op jit(solution)/shard_map/ppermute | solution.py:565
  417.5 13.8 %collective-permute-start.37 = (s16[400,384]{1,0:T(8,128)(2,1)S(1)}, s16[400,384]{1,0:T(8,128)(2,1)S(1)}, u32[]{:S(2)}, u32[]{:S(2)}) collective-permute-start(s16[400,384]{1,0:T(8,128)(2,1)S(1)} %get-tuple-element.89), channel_id=1, source_target_pairs={{0,4},{2,6},{4,0},{6,2},{8,12},{10,14},{12,8},{14,10},{16,20},{18,... | collective-permute-start | bytes 921608 | tf_op jit(solution)/shard_map/ppermute | solution.py:565
  419.8 27.5 %collective-permute-start.49 = (s16[2,400,384]{2,1,0:T(8,128)(2,1)S(1)}, s16[2,400,384]{2,1,0:T(8,128)(2,1)}, u32[]{:S(2)}, u32[]{:S(2)}) collective-permute-start(s16[2,400,384]{2,1,0:T(8,128)(2,1)S(1)} %add_line.4), channel_id=1, source_target_pairs={{0,8},{2,10},{4,12},{6,14},{8,0},{10,2},{12,4},{14,6},{16,24},{18,... | collective-permute-start | bytes 1843208 | tf_op jit(solution)/shard_map/ppermute | solution.py:565
  424.1 31.8 %collective-permute-start.29 = (s16[2,400,384]{2,1,0:T(8,128)(2,1)}, s16[2,400,384]{2,1,0:T(8,128)(2,1)}, u32[]{:S(2)}, u32[]{:S(2)}) collective-permute-start(s16[2,400,384]{2,1,0:T(8,128)(2,1)} %get-tuple-element.73), channel_id=1, source_target_pairs={{0,4},{2,6},{4,0},{6,2},{8,12},{10,14},{12,8},{14,10},{16,20},{18,... | collective-permute-start | bytes 1843208 | tf_op jit(solution)/shard_map/ppermute | solution.py:565
  425.2 30.8 %collective-permute-start.30 = (s16[2,400,384]{2,1,0:T(8,128)(2,1)}, s16[2,400,384]{2,1,0:T(8,128)(2,1)}, u32[]{:S(2)}, u32[]{:S(2)}) collective-permute-start(s16[2,400,384]{2,1,0:T(8,128)(2,1)} %get-tuple-element.75), channel_id=1, source_target_pairs={{0,2},{2,0},{4,6},{6,4},{8,10},{10,8},{12,14},{14,12},{16,18},{18,... | collective-permute-start | bytes 1843208 | tf_op jit(solution)/shard_map/ppermute | solution.py:565
  430.8 14.8 %collective-permute-start.42 = (s16[400,384]{1,0:T(8,128)(2,1)}, s16[400,384]{1,0:T(8,128)(2,1)S(1)}, u32[]{:S(2)}, u32[]{:S(2)}) collective-permute-start(s16[400,384]{1,0:T(8,128)(2,1)} %get-tuple-element.97), channel_id=1, source_target_pairs={{0,2},{2,0},{4,6},{6,4},{8,10},{10,8},{12,14},{14,12},{16,18},{18,... | collective-permute-start | bytes 921608 | tf_op jit(solution)/shard_map/ppermute | solution.py:565
  432.1 15.2 %collective-permute-start.43 = (s16[400,384]{1,0:T(8,128)(2,1)}, s16[400,384]{1,0:T(8,128)(2,1)}, u32[]{:S(2)}, u32[]{:S(2)}) collective-permute-start(s16[400,384]{1,0:T(8,128)(2,1)} %get-tuple-element.99), channel_id=1, source_target_pairs={{0,4},{2,6},{4,0},{6,2},{8,12},{10,14},{12,8},{14,10},{16,20},{18,... | collective-permute-start | bytes 921608 | tf_op jit(solution)/shard_map/ppermute | solution.py:565
  446.3 22.0 %collective-permute-start.38 = (s16[2,400,384]{2,1,0:T(8,128)(2,1)S(1)}, s16[2,400,384]{2,1,0:T(8,128)(2,1)S(1)}, u32[]{:S(2)}, u32[]{:S(2)}) collective-permute-start(s16[2,400,384]{2,1,0:T(8,128)(2,1)S(1)} %add_line.3), channel_id=1, source_target_pairs={{0,8},{2,10},{4,12},{6,14},{8,0},{10,2},{12,4},{14,6},{16,24},{18,... | collective-permute-start | bytes 1843208 | tf_op jit(solution)/shard_map/ppermute | solution.py:565
  453.0 27.0 %collective-permute-start.50 = (s16[2,400,384]{2,1,0:T(8,128)(2,1)}, s16[2,400,384]{2,1,0:T(8,128)(2,1)S(1)}, u32[]{:S(2)}, u32[]{:S(2)}) collective-permute-start(s16[2,400,384]{2,1,0:T(8,128)(2,1)} %add_line.5), channel_id=1, source_target_pairs={{0,16},{2,18},{4,20},{6,22},{8,24},{10,26},{12,28},{14,30},{16,0},... | collective-permute-start | bytes 1843208 | tf_op jit(solution)/shard_map/ppermute | solution.py:565
  459.8 7.1 %collective-permute-start.31 = (s16[400,384]{1,0:T(8,128)(2,1)}, s16[400,384]{1,0:T(8,128)(2,1)S(1)}, u32[]{:S(2)}, u32[]{:S(2)}) collective-permute-start(s16[400,384]{1,0:T(8,128)(2,1)} %get-tuple-element.77), channel_id=1, source_target_pairs={{0,2},{2,0},{4,6},{6,4},{8,10},{10,8},{12,14},{14,12},{16,18},{18,... | collective-permute-start | bytes 921608 | tf_op jit(solution)/shard_map/ppermute | solution.py:565
  461.3 7.1 %collective-permute-start.32 = (s16[400,384]{1,0:T(8,128)(2,1)}, s16[400,384]{1,0:T(8,128)(2,1)S(1)}, u32[]{:S(2)}, u32[]{:S(2)}) collective-permute-start(s16[400,384]{1,0:T(8,128)(2,1)} %get-tuple-element.79), channel_id=1, source_target_pairs={{0,4},{2,6},{4,0},{6,2},{8,12},{10,14},{12,8},{14,10},{16,20},{18,... | collective-permute-start | bytes 921608 | tf_op jit(solution)/shard_map/ppermute | solution.py:565
  463.6 1.3 collective-permute-start.56
  465.0 21.7 %collective-permute-start.57 = (f32[24,768]{1,0:T(8,128)S(1)}, f32[24,768]{1,0:T(8,128)S(1)}, u32[]{:S(2)}, u32[]{:S(2)}) collective-permute-start(f32[24,768]{1,0:T(8,128)S(1)} %add.554), channel_id=1, source_target_pairs={{0,2},{2,0},{4,6},{6,4},{8,10},{10,8},{12,14},{14,12},{16,18},{18,... | collective-permute-start | bytes 221192 | tf_op jit(solution)/shard_map/ppermute | solution.py:565
  486.6 1.5 collective-permute-start.51
  486.7 4.7 collective-permute-start.58
  488.1 3.6 collective-permute-start.52
  491.4 4.4 collective-permute-start.59
  491.7 4.6 collective-permute-start.53
  495.9 5.5 %collective-permute-start.60 = (f32[24,768]{1,0:T(8,128)S(1)}, f32[24,768]{1,0:T(8,128)S(1)}, u32[]{:S(2)}, u32[]{:S(2)}) collective-permute-start(f32[24,768]{1,0:T(8,128)S(1)} %add.557), channel_id=1, source_target_pairs={{0,16},{2,18},{4,20},{6,22},{8,24},{10,26},{12,28},{14,30},{16,0},... | collective-permute-start | bytes 221192 | tf_op jit(solution)/shard_map/ppermute | solution.py:565
  496.3 5.1 collective-permute-start.54
  501.4 4.6 collective-permute-start.55
  (66 other events, 697.9 us)
